TPU v7x, 32 devices: a whole 2x2x4 slice. The times are simulated.
32 devices in a mesh: sec: 4 (over x, core), rows: 8 (over z, y).
Axes of the slice: x: 2, y: 2, z: 4, core: 2. Of those that a mesh axis runs over, the one named last changes fastest.
Arguments:
- streams: bfloat16 [4, 2, 16, 64, 256], P('sec', None, 'rows'), may hold values from -6 to 6
- cotangents: bfloat16 [4, 2, 16, 64, 256], P('sec', None, 'rows'), may hold values from -6 to 6
- weights: bfloat16 [4, 1, 2, 3, 3, 256, 256], P('sec'), may hold values from -0.125 to 0.125
Outputs:
- input_streams: bfloat16 [4, 2, 16, 64, 256], P('sec', None, 'rows')
- input_grads: bfloat16 [4, 2, 16, 64, 256], P('sec', None, 'rows')
- weight_grads: float32 [4, 4608, 256], P('sec', 'rows')
All inputs are finite; a program needn't handle non-finite values.
Results may differ from a plain program's by a relative error of at most 0.019.
Values may be sent and summed in bfloat16 or wider, within the bound.
A program may use at most 64 MiB of HBM per device.

v0:
```python
import jax
import jax.numpy as jnp
from jax import lax
from jax.sharding import PartitionSpec as P


def with_halo(shard, sides, width):
    for axis, dim in sides:
        size, length = (lax.axis_size(axis), shard.shape[dim])
        up = [(i, (i + 1) % size) for i in range(size - 1)]
        down = [(j, i) for i, j in up]
        last = lax.slice_in_dim(shard, length - width, length, axis=dim)
        initial = lax.slice_in_dim(shard, 0, width, axis=dim)
        before = lax.ppermute(last, axis, up)
        after = lax.ppermute(initial, axis, down)
        shard = jnp.concatenate([before, shard, after], axis=dim)
    return shard


def from_behind(shard, axis, by):
    size = lax.axis_size(axis)
    pairs = [(i, i + by) for i in range(size) if 0 <= i + by < size]
    return lax.ppermute(shard, axis, pairs)


def conv_rows(field, kernel):
    return lax.conv_general_dilated(
        field[None],
        kernel,
        (1, 1),
        ((0, 0), (1, 1)),
        dimension_numbers=("NHWC", "HWIO", "NHWC"),
        preferred_element_type=jnp.float32,
    )[0]


def silu_slope(value):
    sig = jax.nn.sigmoid(value)
    return sig + value * sig * (1.0 - sig)


def tap_grads(act, cotan):
    padded = jnp.pad(act, ((0, 0), (1, 1), (0, 0)))
    height, width = (cotan.shape[0], cotan.shape[1])
    patches = jnp.stack(
        [
            padded[row_tap : row_tap + height, col_tap : col_tap + width]
            for row_tap in range(3)
            for col_tap in range(3)
        ]
    )
    summed = lax.dot_general(
        patches, cotan, (((1, 2), (0, 1)), ((), ())), preferred_element_type=jnp.float32
    )
    return summed.reshape(3, 3, act.shape[-1], cotan.shape[-1])


def deep_layer(state, kernel_f, kernel_g, turned_f, turned_g, inside):
    full = with_halo(state, (("rows", 1),), 2)
    keep = inside[:, None, None]
    act_g = jax.nn.silu(full[0].astype(jnp.float32)).astype(jnp.bfloat16)
    upper_wide = full[0, 1:-1].astype(jnp.float32)
    lower_in = jnp.where(
        keep, full[1, 1:-1].astype(jnp.float32) - conv_rows(act_g, kernel_g), 0.0
    ).astype(jnp.bfloat16)
    carried = jnp.where(
        keep,
        full[2, 1:-1].astype(jnp.float32) + conv_rows(full[3], turned_g) * silu_slope(upper_wide),
        0.0,
    ).astype(jnp.bfloat16)
    grad_g = tap_grads(act_g[1:-1], state[3])
    act_f = jax.nn.silu(lower_in.astype(jnp.float32)).astype(jnp.bfloat16)
    upper_in = (state[0].astype(jnp.float32) - conv_rows(act_f, kernel_f)).astype(jnp.bfloat16)
    lower_own = lower_in[1:-1]
    grad_lower_in = (
        state[3].astype(jnp.float32)
        + conv_rows(carried, turned_f) * silu_slope(lower_own.astype(jnp.float32))
    ).astype(jnp.bfloat16)
    grad_f = tap_grads(act_f, carried[1:-1])
    return (jnp.stack([upper_in, lower_own, carried[1:-1], grad_lower_in]), grad_f, grad_g)


def local(streams, cotangents, weights):
    sec_pos = lax.axis_index("sec")
    sections = lax.axis_size("sec")
    kernels = weights[0]
    turned = jnp.flip(kernels, (2, 3)).swapaxes(4, 5)
    layers = kernels.shape[0]
    all_streams, all_cotangents = (
        lax.all_gather(streams, "sec", axis=0, tiled=True),
        lax.all_gather(cotangents, "sec", axis=0, tiled=True),
    )
    crops = all_streams.shape[0]
    height_dev = streams.shape[2]
    columns = streams.shape[3]
    channels = streams.shape[4]
    ticks = crops + sections - 1
    scale = (crops * height_dev * lax.axis_size("rows") * columns) ** (-0.5)
    row_global = lax.axis_index("rows") * height_dev + jnp.arange(-1, height_dev + 1)
    inside = (row_global >= 0) & (row_global < height_dev * lax.axis_size("rows"))
    term_rows = layers * 18 * channels
    grads_start = jnp.zeros((layers, 2, 3, 3, channels, channels), jnp.float32)
    state_start = jnp.zeros((4, height_dev, columns, channels), jnp.bfloat16)
    finished_start = jnp.zeros((crops, 4, height_dev, columns, channels), jnp.bfloat16)

    def tick_step(tick, carry):
        state, grads, finished = carry
        arrived = from_behind(state, "sec", -1)
        pick = jnp.clip(tick, 0, crops - 1)
        top = jnp.concatenate(
            [
                lax.dynamic_index_in_dim(all_streams, pick, 0, False),
                lax.dynamic_index_in_dim(all_cotangents, pick, 0, False),
            ],
            0,
        )
        state = jnp.where(sec_pos == sections - 1, top, arrived)
        crop_here = tick - (sections - 1 - sec_pos)
        valid = (crop_here >= 0) & (crop_here < crops)
        factor = jnp.where(valid, scale, 0.0).astype(jnp.float32)
        collected = []
        for layer in reversed(range(layers)):
            state, grad_f, grad_g = deep_layer(
                state,
                kernels[layer, 0],
                kernels[layer, 1],
                turned[layer, 0],
                turned[layer, 1],
                inside,
            )
            collected = [jnp.stack([grad_f, grad_g]) * factor] + collected
        grads = grads + jnp.stack(collected)
        slot = jnp.clip(tick - (sections - 1), 0, crops - 1)
        previous = lax.dynamic_index_in_dim(finished, slot, 0, False)
        chosen = jnp.where((sec_pos == 0) & valid, state, previous)
        finished = lax.dynamic_update_index_in_dim(finished, chosen, slot, 0)
        return (state, grads, finished)

    state, grads, finished = lax.fori_loop(
        0, ticks, tick_step, (state_start, grads_start, finished_start)
    )
    shards = lax.psum_scatter(
        grads.reshape(term_rows, channels), "rows", scatter_dimension=0, tiled=True
    )
    delivered = lax.psum_scatter(
        finished.astype(jnp.float32).astype(jnp.bfloat16), "sec", scatter_dimension=0, tiled=True
    )
    return (delivered[:, :2], delivered[:, 2:], shards[None])


def solution(mesh):
    placed = (
        P("sec", None, "rows", None, None),
        P("sec", None, "rows", None, None),
        P("sec", None, None, None, None, None, None),
    )
    return jax.shard_map(
        local,
        mesh=mesh,
        in_specs=placed,
        out_specs=(
            P("sec", None, "rows", None, None),
            P("sec", None, "rows", None, None),
            P("sec", "rows", None),
        ),
        check_vma=False,
    )
```

profile of v0, /device:TPU:0, one launch (start us, length us, event | category | flops | bytes accessed | tf_op | source)
XLA Modules:
  0.0 376.1 jit_solution(11029591678256203457)
XLA Ops:
  7.2 8.8 %all_gather.6 = bf16[4,2,2,64,256]{4,3,2,1,0:T(8,128)(2,1)S(1)} all-gather(bf16[1,2,2,64,256]{4,3,2,1,0:T(8,128)(2,1)} %param.5), channel_id=1, replica_groups=mesh['sec'=4,'rows'=8] {'sec'}, dimensions={0}, use_global_device_ids=true | all-gather | bytes 655360 | tf_op jit(solution)/shard_map/all_gather | solution.py:90
  16.1 7.5 %all_gather.7 = bf16[4,2,2,64,256]{4,3,2,1,0:T(8,128)(2,1)S(1)} all-gather(bf16[1,2,2,64,256]{4,3,2,1,0:T(8,128)(2,1)} %param.6), channel_id=1, replica_groups=mesh['sec'=4,'rows'=8] {'sec'}, dimensions={0}, use_global_device_ids=true | all-gather | bytes 655360 | tf_op jit(solution)/shard_map/all_gather | solution.py:91
  23.5 2.8 copy.48
  28.2 210.2 %while.20 = (s32[]{:T(128)}, bf16[4,2,64,256]{3,2,1,0:T(8,128)(2,1)S(1)}, f32[1,2,3,3,256,256]{5,4,3,2,1,0:T(8,128)}, bf16[4,4,2,64,256]{4,3,2,1,0:T(8,128)(2,1)...) while((s32[]{:T(128)}, ...), condition=%wide.region_1.2_spmd.clone, body=%wide.region_0.1_spmd.clone.sunk | while | flops 1336811520 | bytes 105808488 | solution.py:139
  31.7 3.4 collective-permute-start.2
  36.5 2.4 collective-permute-done.2
  39.0 4.4 %collective-permute-done.1 = bf16[4,2,64,256]{3,2,1,0:T(8,128)(2,1)S(1)} collective-permute-done((bf16[4,2,64,256]{3,2,1,0:T(8,128)(2,1)S(1)}, bf16[4,2,64,256]{3,2,1,0:T(8,128)(2,1)S(1)}, u32[]{:S(2)}, u32[]{:S(2)}) %collective-permute-start.1) | collective-permute-done | bytes 262176 | tf_op jit(solution)/shard_map/while/body/eval_jaxpr/ppermute | solution.py:15
  55.0 6.6 %collective-permute-done = bf16[4,2,64,256]{3,2,1,0:T(8,128)(2,1)S(1)} collective-permute-done((bf16[4,2,64,256]{3,2,1,0:T(8,128)(2,1)S(1)}, bf16[4,2,64,256]{3,2,1,0:T(8,128)(2,1)S(1)}, u32[]{:S(2)}, u32[]{:S(2)}) %collective-permute-start) | collective-permute-done | bytes 262176 | tf_op jit(solution)/shard_map/while/body/eval_jaxpr/ppermute | solution.py:23
  61.6 4.1 %collective-permute-start.2 = (bf16[4,2,64,256]{3,2,1,0:T(8,128)(2,1)S(1)}, bf16[4,2,64,256]{3,2,1,0:T(8,128)(2,1)S(1)}, u32[]{:S(2)}, u32[]{:S(2)}) collective-permute-start(bf16[4,2,64,256]{3,2,1,0:T(8,128)(2,1)S(1)} %maximum_select_fusion.3), channel_id=1, source_target_pairs={{0,1},{1,2},{2,3},{3,4},{4,5},{5,6},{6,7},{8,9},{9,10},{10,11},{11... | collective-permute-start | bytes 786440 | tf_op jit(solution)/shard_map/while/body/eval_jaxpr/ppermute | solution.py:14
  67.2 2.4 collective-permute-done.2
  69.6 4.4 %collective-permute-done.1 = bf16[4,2,64,256]{3,2,1,0:T(8,128)(2,1)S(1)} collective-permute-done((bf16[4,2,64,256]{3,2,1,0:T(8,128)(2,1)S(1)}, bf16[4,2,64,256]{3,2,1,0:T(8,128)(2,1)S(1)}, u32[]{:S(2)}, u32[]{:S(2)}) %collective-permute-start.1) | collective-permute-done | bytes 262176 | tf_op jit(solution)/shard_map/while/body/eval_jaxpr/ppermute | solution.py:15
  85.7 6.7 %collective-permute-done = bf16[4,2,64,256]{3,2,1,0:T(8,128)(2,1)S(1)} collective-permute-done((bf16[4,2,64,256]{3,2,1,0:T(8,128)(2,1)S(1)}, bf16[4,2,64,256]{3,2,1,0:T(8,128)(2,1)S(1)}, u32[]{:S(2)}, u32[]{:S(2)}) %collective-permute-start) | collective-permute-done | bytes 262176 | tf_op jit(solution)/shard_map/while/body/eval_jaxpr/ppermute | solution.py:23
  92.4 4.1 %collective-permute-start.2 = (bf16[4,2,64,256]{3,2,1,0:T(8,128)(2,1)S(1)}, bf16[4,2,64,256]{3,2,1,0:T(8,128)(2,1)S(1)}, u32[]{:S(2)}, u32[]{:S(2)}) collective-permute-start(bf16[4,2,64,256]{3,2,1,0:T(8,128)(2,1)S(1)} %maximum_select_fusion.3), channel_id=1, source_target_pairs={{0,1},{1,2},{2,3},{3,4},{4,5},{5,6},{6,7},{8,9},{9,10},{10,11},{11... | collective-permute-start | bytes 786440 | tf_op jit(solution)/shard_map/while/body/eval_jaxpr/ppermute | solution.py:14
  98.0 2.4 collective-permute-done.2
  100.4 4.4 %collective-permute-done.1 = bf16[4,2,64,256]{3,2,1,0:T(8,128)(2,1)S(1)} collective-permute-done((bf16[4,2,64,256]{3,2,1,0:T(8,128)(2,1)S(1)}, bf16[4,2,64,256]{3,2,1,0:T(8,128)(2,1)S(1)}, u32[]{:S(2)}, u32[]{:S(2)}) %collective-permute-start.1) | collective-permute-done | bytes 262176 | tf_op jit(solution)/shard_map/while/body/eval_jaxpr/ppermute | solution.py:15
  116.5 6.7 %collective-permute-done = bf16[4,2,64,256]{3,2,1,0:T(8,128)(2,1)S(1)} collective-permute-done((bf16[4,2,64,256]{3,2,1,0:T(8,128)(2,1)S(1)}, bf16[4,2,64,256]{3,2,1,0:T(8,128)(2,1)S(1)}, u32[]{:S(2)}, u32[]{:S(2)}) %collective-permute-start) | collective-permute-done | bytes 262176 | tf_op jit(solution)/shard_map/while/body/eval_jaxpr/ppermute | solution.py:23
  123.2 4.1 %collective-permute-start.2 = (bf16[4,2,64,256]{3,2,1,0:T(8,128)(2,1)S(1)}, bf16[4,2,64,256]{3,2,1,0:T(8,128)(2,1)S(1)}, u32[]{:S(2)}, u32[]{:S(2)}) collective-permute-start(bf16[4,2,64,256]{3,2,1,0:T(8,128)(2,1)S(1)} %maximum_select_fusion.3), channel_id=1, source_target_pairs={{0,1},{1,2},{2,3},{3,4},{4,5},{5,6},{6,7},{8,9},{9,10},{10,11},{11... | collective-permute-start | bytes 786440 | tf_op jit(solution)/shard_map/while/body/eval_jaxpr/ppermute | solution.py:14
  128.7 2.4 collective-permute-done.2
  131.2 4.4 %collective-permute-done.1 = bf16[4,2,64,256]{3,2,1,0:T(8,128)(2,1)S(1)} collective-permute-done((bf16[4,2,64,256]{3,2,1,0:T(8,128)(2,1)S(1)}, bf16[4,2,64,256]{3,2,1,0:T(8,128)(2,1)S(1)}, u32[]{:S(2)}, u32[]{:S(2)}) %collective-permute-start.1) | collective-permute-done | bytes 262176 | tf_op jit(solution)/shard_map/while/body/eval_jaxpr/ppermute | solution.py:15
  147.3 6.7 %collective-permute-done = bf16[4,2,64,256]{3,2,1,0:T(8,128)(2,1)S(1)} collective-permute-done((bf16[4,2,64,256]{3,2,1,0:T(8,128)(2,1)S(1)}, bf16[4,2,64,256]{3,2,1,0:T(8,128)(2,1)S(1)}, u32[]{:S(2)}, u32[]{:S(2)}) %collective-permute-start) | collective-permute-done | bytes 262176 | tf_op jit(solution)/shard_map/while/body/eval_jaxpr/ppermute | solution.py:23
  154.0 4.1 %collective-permute-start.2 = (bf16[4,2,64,256]{3,2,1,0:T(8,128)(2,1)S(1)}, bf16[4,2,64,256]{3,2,1,0:T(8,128)(2,1)S(1)}, u32[]{:S(2)}, u32[]{:S(2)}) collective-permute-start(bf16[4,2,64,256]{3,2,1,0:T(8,128)(2,1)S(1)} %maximum_select_fusion.3), channel_id=1, source_target_pairs={{0,1},{1,2},{2,3},{3,4},{4,5},{5,6},{6,7},{8,9},{9,10},{10,11},{11... | collective-permute-start | bytes 786440 | tf_op jit(solution)/shard_map/while/body/eval_jaxpr/ppermute | solution.py:14
  159.5 2.4 collective-permute-done.2
  162.0 4.4 %collective-permute-done.1 = bf16[4,2,64,256]{3,2,1,0:T(8,128)(2,1)S(1)} collective-permute-done((bf16[4,2,64,256]{3,2,1,0:T(8,128)(2,1)S(1)}, bf16[4,2,64,256]{3,2,1,0:T(8,128)(2,1)S(1)}, u32[]{:S(2)}, u32[]{:S(2)}) %collective-permute-start.1) | collective-permute-done | bytes 262176 | tf_op jit(solution)/shard_map/while/body/eval_jaxpr/ppermute | solution.py:15
  178.1 6.7 %collective-permute-done = bf16[4,2,64,256]{3,2,1,0:T(8,128)(2,1)S(1)} collective-permute-done((bf16[4,2,64,256]{3,2,1,0:T(8,128)(2,1)S(1)}, bf16[4,2,64,256]{3,2,1,0:T(8,128)(2,1)S(1)}, u32[]{:S(2)}, u32[]{:S(2)}) %collective-permute-start) | collective-permute-done | bytes 262176 | tf_op jit(solution)/shard_map/while/body/eval_jaxpr/ppermute | solution.py:23
  184.8 4.1 %collective-permute-start.2 = (bf16[4,2,64,256]{3,2,1,0:T(8,128)(2,1)S(1)}, bf16[4,2,64,256]{3,2,1,0:T(8,128)(2,1)S(1)}, u32[]{:S(2)}, u32[]{:S(2)}) collective-permute-start(bf16[4,2,64,256]{3,2,1,0:T(8,128)(2,1)S(1)} %maximum_select_fusion.3), channel_id=1, source_target_pairs={{0,1},{1,2},{2,3},{3,4},{4,5},{5,6},{6,7},{8,9},{9,10},{10,11},{11... | collective-permute-start | bytes 786440 | tf_op jit(solution)/shard_map/while/body/eval_jaxpr/ppermute | solution.py:14
  190.3 2.4 collective-permute-done.2
  192.8 4.4 %collective-permute-done.1 = bf16[4,2,64,256]{3,2,1,0:T(8,128)(2,1)S(1)} collective-permute-done((bf16[4,2,64,256]{3,2,1,0:T(8,128)(2,1)S(1)}, bf16[4,2,64,256]{3,2,1,0:T(8,128)(2,1)S(1)}, u32[]{:S(2)}, u32[]{:S(2)}) %collective-permute-start.1) | collective-permute-done | bytes 262176 | tf_op jit(solution)/shard_map/while/body/eval_jaxpr/ppermute | solution.py:15
  208.9 6.7 %collective-permute-done = bf16[4,2,64,256]{3,2,1,0:T(8,128)(2,1)S(1)} collective-permute-done((bf16[4,2,64,256]{3,2,1,0:T(8,128)(2,1)S(1)}, bf16[4,2,64,256]{3,2,1,0:T(8,128)(2,1)S(1)}, u32[]{:S(2)}, u32[]{:S(2)}) %collective-permute-start) | collective-permute-done | bytes 262176 | tf_op jit(solution)/shard_map/while/body/eval_jaxpr/ppermute | solution.py:23
  215.6 4.1 %collective-permute-start.2 = (bf16[4,2,64,256]{3,2,1,0:T(8,128)(2,1)S(1)}, bf16[4,2,64,256]{3,2,1,0:T(8,128)(2,1)S(1)}, u32[]{:S(2)}, u32[]{:S(2)}) collective-permute-start(bf16[4,2,64,256]{3,2,1,0:T(8,128)(2,1)S(1)} %maximum_select_fusion.3), channel_id=1, source_target_pairs={{0,1},{1,2},{2,3},{3,4},{4,5},{5,6},{6,7},{8,9},{9,10},{10,11},{11... | collective-permute-start | bytes 786440 | tf_op jit(solution)/shard_map/while/body/eval_jaxpr/ppermute | solution.py:14
  223.6 4.4 %collective-permute-done.1 = bf16[4,2,64,256]{3,2,1,0:T(8,128)(2,1)S(1)} collective-permute-done((bf16[4,2,64,256]{3,2,1,0:T(8,128)(2,1)S(1)}, bf16[4,2,64,256]{3,2,1,0:T(8,128)(2,1)S(1)}, u32[]{:S(2)}, u32[]{:S(2)}) %collective-permute-start.1) | collective-permute-done | bytes 262176 | tf_op jit(solution)/shard_map/while/body/eval_jaxpr/ppermute | solution.py:15
  240.1 29.0 %reduce-scatter.3.cloned.1.call-done = bf16[1,4,2,64,256]{4,3,2,1,0:T(8,128)(2,1)} async-done(((bf16[4,4,2,64,256]{4,3,2,1,0:T(8,128)(2,1)}), bf16[1,4,2,64,256]{4,3,2,1,0:T(8,128)(2,1)}) %reduce-scatter.3.cloned.1.call-update) | async-done | bytes 262160 | tf_op jit(solution)/shard_map/reduce_scatter | solution.py:145
  270.8 98.5 %reduce-scatter.5.cloned.1.call-done = f32[576,256]{1,0:T(8,128)} async-done(((f32[4608,256]{1,0:T(8,128)}), f32[576,256]{1,0:T(8,128)}) %reduce-scatter.5.cloned.1.call-update) | async-done | bytes 589840 | tf_op jit(solution)/shard_map/reduce_scatter | solution.py:142
  (589 shorter events, 97.6 us)
Async XLA Ops:
  7.2 262.0 %reduce-scatter.3.cloned.1.call-start = ((), (), s32[]{:S(2)}) async-start(), calls=%async_computation.2 | async-start | bytes 1310720 | tf_op jit(solution)/shard_map/reduce_scatter | solution.py:145
  28.2 3.4 collective-permute-start
  31.7 7.3 %collective-permute-start.2 = (bf16[4,2,64,256]{3,2,1,0:T(8,128)(2,1)S(1)}, bf16[4,2,64,256]{3,2,1,0:T(8,128)(2,1)S(1)}, u32[]{:S(2)}, u32[]{:S(2)}) collective-permute-start(bf16[4,2,64,256]{3,2,1,0:T(8,128)(2,1)S(1)} %maximum_select_fusion.3), channel_id=1, source_target_pairs={{0,1},{1,2},{2,3},{3,4},{4,5},{5,6},{6,7},{8,9},{9,10},{10,11},{11... | collective-permute-start | bytes 786440 | tf_op jit(solution)/shard_map/while/body/eval_jaxpr/ppermute | solution.py:14
  35.1 8.3 %collective-permute-start.1 = (bf16[4,2,64,256]{3,2,1,0:T(8,128)(2,1)S(1)}, bf16[4,2,64,256]{3,2,1,0:T(8,128)(2,1)S(1)}, u32[]{:S(2)}, u32[]{:S(2)}) collective-permute-start(bf16[4,2,64,256]{3,2,1,0:T(8,128)(2,1)S(1)} %maximum_select_fusion.3), channel_id=1, source_target_pairs={{1,0},{2,1},{3,2},{4,3},{5,4},{6,5},{7,6},{9,8},{10,9},{11,10},{12... | collective-permute-start | bytes 786440 | tf_op jit(solution)/shard_map/while/body/eval_jaxpr/ppermute | solution.py:15
  36.5 7.5 %copy-start.3 = (bf16[1,2,3,3,256,256]{5,4,3,2,1,0:T(8,128)(2,1)S(1)}, bf16[1,2,3,3,256,256]{5,4,3,2,1,0:T(8,128)(2,1)}, u32[]{:S(2)}) copy-start(bf16[1,2,3,3,256,256]{5,4,3,2,1,0:T(8,128)(2,1)} %get-tuple-element.499) | copy-start | bytes 7077892 | tf_op jit(solution)/shard_map/while
  53.7 7.9 %collective-permute-start = (bf16[4,2,64,256]{3,2,1,0:T(8,128)(2,1)S(1)}, bf16[4,2,64,256]{3,2,1,0:T(8,128)(2,1)S(1)}, u32[]{:S(2)}, u32[]{:S(2)}) collective-permute-start(bf16[4,2,64,256]{3,2,1,0:T(8,128)(2,1)S(1)} %get-tuple-element.471), channel_id=1, source_target_pairs={{8,0},{16,8},{24,16},{9,1},{17,9},{25,17},{10,2},{18,10},{26,18},{... | collective-permute-start | bytes 786440 | tf_op jit(solution)/shard_map/while/body/eval_jaxpr/ppermute | solution.py:23
  61.6 8.0 %collective-permute-start.2 = (bf16[4,2,64,256]{3,2,1,0:T(8,128)(2,1)S(1)}, bf16[4,2,64,256]{3,2,1,0:T(8,128)(2,1)S(1)}, u32[]{:S(2)}, u32[]{:S(2)}) collective-permute-start(bf16[4,2,64,256]{3,2,1,0:T(8,128)(2,1)S(1)} %maximum_select_fusion.3), channel_id=1, source_target_pairs={{0,1},{1,2},{2,3},{3,4},{4,5},{5,6},{6,7},{8,9},{9,10},{10,11},{11... | collective-permute-start | bytes 786440 | tf_op jit(solution)/shard_map/while/body/eval_jaxpr/ppermute | solution.py:14
  65.7 8.3 %collective-permute-start.1 = (bf16[4,2,64,256]{3,2,1,0:T(8,128)(2,1)S(1)}, bf16[4,2,64,256]{3,2,1,0:T(8,128)(2,1)S(1)}, u32[]{:S(2)}, u32[]{:S(2)}) collective-permute-start(bf16[4,2,64,256]{3,2,1,0:T(8,128)(2,1)S(1)} %maximum_select_fusion.3), channel_id=1, source_target_pairs={{1,0},{2,1},{3,2},{4,3},{5,4},{6,5},{7,6},{9,8},{10,9},{11,10},{12... | collective-permute-start | bytes 786440 | tf_op jit(solution)/shard_map/while/body/eval_jaxpr/ppermute | solution.py:15
  67.2 7.5 %copy-start.3 = (bf16[1,2,3,3,256,256]{5,4,3,2,1,0:T(8,128)(2,1)S(1)}, bf16[1,2,3,3,256,256]{5,4,3,2,1,0:T(8,128)(2,1)}, u32[]{:S(2)}) copy-start(bf16[1,2,3,3,256,256]{5,4,3,2,1,0:T(8,128)(2,1)} %get-tuple-element.499) | copy-start | bytes 7077892 | tf_op jit(solution)/shard_map/while
  84.3 8.0 %collective-permute-start = (bf16[4,2,64,256]{3,2,1,0:T(8,128)(2,1)S(1)}, bf16[4,2,64,256]{3,2,1,0:T(8,128)(2,1)S(1)}, u32[]{:S(2)}, u32[]{:S(2)}) collective-permute-start(bf16[4,2,64,256]{3,2,1,0:T(8,128)(2,1)S(1)} %get-tuple-element.471), channel_id=1, source_target_pairs={{8,0},{16,8},{24,16},{9,1},{17,9},{25,17},{10,2},{18,10},{26,18},{... | collective-permute-start | bytes 786440 | tf_op jit(solution)/shard_map/while/body/eval_jaxpr/ppermute | solution.py:23
  92.4 8.0 %collective-permute-start.2 = (bf16[4,2,64,256]{3,2,1,0:T(8,128)(2,1)S(1)}, bf16[4,2,64,256]{3,2,1,0:T(8,128)(2,1)S(1)}, u32[]{:S(2)}, u32[]{:S(2)}) collective-permute-start(bf16[4,2,64,256]{3,2,1,0:T(8,128)(2,1)S(1)} %maximum_select_fusion.3), channel_id=1, source_target_pairs={{0,1},{1,2},{2,3},{3,4},{4,5},{5,6},{6,7},{8,9},{9,10},{10,11},{11... | collective-permute-start | bytes 786440 | tf_op jit(solution)/shard_map/while/body/eval_jaxpr/ppermute | solution.py:14
  96.5 8.3 %collective-permute-start.1 = (bf16[4,2,64,256]{3,2,1,0:T(8,128)(2,1)S(1)}, bf16[4,2,64,256]{3,2,1,0:T(8,128)(2,1)S(1)}, u32[]{:S(2)}, u32[]{:S(2)}) collective-permute-start(bf16[4,2,64,256]{3,2,1,0:T(8,128)(2,1)S(1)} %maximum_select_fusion.3), channel_id=1, source_target_pairs={{1,0},{2,1},{3,2},{4,3},{5,4},{6,5},{7,6},{9,8},{10,9},{11,10},{12... | collective-permute-start | bytes 786440 | tf_op jit(solution)/shard_map/while/body/eval_jaxpr/ppermute | solution.py:15
  97.9 7.5 %copy-start.3 = (bf16[1,2,3,3,256,256]{5,4,3,2,1,0:T(8,128)(2,1)S(1)}, bf16[1,2,3,3,256,256]{5,4,3,2,1,0:T(8,128)(2,1)}, u32[]{:S(2)}) copy-start(bf16[1,2,3,3,256,256]{5,4,3,2,1,0:T(8,128)(2,1)} %get-tuple-element.499) | copy-start | bytes 7077892 | tf_op jit(solution)/shard_map/while
  115.1 8.0 %collective-permute-start = (bf16[4,2,64,256]{3,2,1,0:T(8,128)(2,1)S(1)}, bf16[4,2,64,256]{3,2,1,0:T(8,128)(2,1)S(1)}, u32[]{:S(2)}, u32[]{:S(2)}) collective-permute-start(bf16[4,2,64,256]{3,2,1,0:T(8,128)(2,1)S(1)} %get-tuple-element.471), channel_id=1, source_target_pairs={{8,0},{16,8},{24,16},{9,1},{17,9},{25,17},{10,2},{18,10},{26,18},{... | collective-permute-start | bytes 786440 | tf_op jit(solution)/shard_map/while/body/eval_jaxpr/ppermute | solution.py:23
  123.2 8.0 %collective-permute-start.2 = (bf16[4,2,64,256]{3,2,1,0:T(8,128)(2,1)S(1)}, bf16[4,2,64,256]{3,2,1,0:T(8,128)(2,1)S(1)}, u32[]{:S(2)}, u32[]{:S(2)}) collective-permute-start(bf16[4,2,64,256]{3,2,1,0:T(8,128)(2,1)S(1)} %maximum_select_fusion.3), channel_id=1, source_target_pairs={{0,1},{1,2},{2,3},{3,4},{4,5},{5,6},{6,7},{8,9},{9,10},{10,11},{11... | collective-permute-start | bytes 786440 | tf_op jit(solution)/shard_map/while/body/eval_jaxpr/ppermute | solution.py:14
  127.3 8.3 %collective-permute-start.1 = (bf16[4,2,64,256]{3,2,1,0:T(8,128)(2,1)S(1)}, bf16[4,2,64,256]{3,2,1,0:T(8,128)(2,1)S(1)}, u32[]{:S(2)}, u32[]{:S(2)}) collective-permute-start(bf16[4,2,64,256]{3,2,1,0:T(8,128)(2,1)S(1)} %maximum_select_fusion.3), channel_id=1, source_target_pairs={{1,0},{2,1},{3,2},{4,3},{5,4},{6,5},{7,6},{9,8},{10,9},{11,10},{12... | collective-permute-start | bytes 786440 | tf_op jit(solution)/shard_map/while/body/eval_jaxpr/ppermute | solution.py:15
  128.7 7.5 %copy-start.3 = (bf16[1,2,3,3,256,256]{5,4,3,2,1,0:T(8,128)(2,1)S(1)}, bf16[1,2,3,3,256,256]{5,4,3,2,1,0:T(8,128)(2,1)}, u32[]{:S(2)}) copy-start(bf16[1,2,3,3,256,256]{5,4,3,2,1,0:T(8,128)(2,1)} %get-tuple-element.499) | copy-start | bytes 7077892 | tf_op jit(solution)/shard_map/while
  140.4 2.4 slice-start
  145.9 8.0 %collective-permute-start = (bf16[4,2,64,256]{3,2,1,0:T(8,128)(2,1)S(1)}, bf16[4,2,64,256]{3,2,1,0:T(8,128)(2,1)S(1)}, u32[]{:S(2)}, u32[]{:S(2)}) collective-permute-start(bf16[4,2,64,256]{3,2,1,0:T(8,128)(2,1)S(1)} %get-tuple-element.471), channel_id=1, source_target_pairs={{8,0},{16,8},{24,16},{9,1},{17,9},{25,17},{10,2},{18,10},{26,18},{... | collective-permute-start | bytes 786440 | tf_op jit(solution)/shard_map/while/body/eval_jaxpr/ppermute | solution.py:23
  154.0 8.0 %collective-permute-start.2 = (bf16[4,2,64,256]{3,2,1,0:T(8,128)(2,1)S(1)}, bf16[4,2,64,256]{3,2,1,0:T(8,128)(2,1)S(1)}, u32[]{:S(2)}, u32[]{:S(2)}) collective-permute-start(bf16[4,2,64,256]{3,2,1,0:T(8,128)(2,1)S(1)} %maximum_select_fusion.3), channel_id=1, source_target_pairs={{0,1},{1,2},{2,3},{3,4},{4,5},{5,6},{6,7},{8,9},{9,10},{10,11},{11... | collective-permute-start | bytes 786440 | tf_op jit(solution)/shard_map/while/body/eval_jaxpr/ppermute | solution.py:14
  158.1 8.3 %collective-permute-start.1 = (bf16[4,2,64,256]{3,2,1,0:T(8,128)(2,1)S(1)}, bf16[4,2,64,256]{3,2,1,0:T(8,128)(2,1)S(1)}, u32[]{:S(2)}, u32[]{:S(2)}) collective-permute-start(bf16[4,2,64,256]{3,2,1,0:T(8,128)(2,1)S(1)} %maximum_select_fusion.3), channel_id=1, source_target_pairs={{1,0},{2,1},{3,2},{4,3},{5,4},{6,5},{7,6},{9,8},{10,9},{11,10},{12... | collective-permute-start | bytes 786440 | tf_op jit(solution)/shard_map/while/body/eval_jaxpr/ppermute | solution.py:15
  159.5 7.5 %copy-start.3 = (bf16[1,2,3,3,256,256]{5,4,3,2,1,0:T(8,128)(2,1)S(1)}, bf16[1,2,3,3,256,256]{5,4,3,2,1,0:T(8,128)(2,1)}, u32[]{:S(2)}) copy-start(bf16[1,2,3,3,256,256]{5,4,3,2,1,0:T(8,128)(2,1)} %get-tuple-element.499) | copy-start | bytes 7077892 | tf_op jit(solution)/shard_map/while
  171.2 2.4 slice-start
  176.7 8.0 %collective-permute-start = (bf16[4,2,64,256]{3,2,1,0:T(8,128)(2,1)S(1)}, bf16[4,2,64,256]{3,2,1,0:T(8,128)(2,1)S(1)}, u32[]{:S(2)}, u32[]{:S(2)}) collective-permute-start(bf16[4,2,64,256]{3,2,1,0:T(8,128)(2,1)S(1)} %get-tuple-element.471), channel_id=1, source_target_pairs={{8,0},{16,8},{24,16},{9,1},{17,9},{25,17},{10,2},{18,10},{26,18},{... | collective-permute-start | bytes 786440 | tf_op jit(solution)/shard_map/while/body/eval_jaxpr/ppermute | solution.py:23
  184.8 8.0 %collective-permute-start.2 = (bf16[4,2,64,256]{3,2,1,0:T(8,128)(2,1)S(1)}, bf16[4,2,64,256]{3,2,1,0:T(8,128)(2,1)S(1)}, u32[]{:S(2)}, u32[]{:S(2)}) collective-permute-start(bf16[4,2,64,256]{3,2,1,0:T(8,128)(2,1)S(1)} %maximum_select_fusion.3), channel_id=1, source_target_pairs={{0,1},{1,2},{2,3},{3,4},{4,5},{5,6},{6,7},{8,9},{9,10},{10,11},{11... | collective-permute-start | bytes 786440 | tf_op jit(solution)/shard_map/while/body/eval_jaxpr/ppermute | solution.py:14
  188.9 8.3 %collective-permute-start.1 = (bf16[4,2,64,256]{3,2,1,0:T(8,128)(2,1)S(1)}, bf16[4,2,64,256]{3,2,1,0:T(8,128)(2,1)S(1)}, u32[]{:S(2)}, u32[]{:S(2)}) collective-permute-start(bf16[4,2,64,256]{3,2,1,0:T(8,128)(2,1)S(1)} %maximum_select_fusion.3), channel_id=1, source_target_pairs={{1,0},{2,1},{3,2},{4,3},{5,4},{6,5},{7,6},{9,8},{10,9},{11,10},{12... | collective-permute-start | bytes 786440 | tf_op jit(solution)/shard_map/while/body/eval_jaxpr/ppermute | solution.py:15
  190.3 7.5 %copy-start.3 = (bf16[1,2,3,3,256,256]{5,4,3,2,1,0:T(8,128)(2,1)S(1)}, bf16[1,2,3,3,256,256]{5,4,3,2,1,0:T(8,128)(2,1)}, u32[]{:S(2)}) copy-start(bf16[1,2,3,3,256,256]{5,4,3,2,1,0:T(8,128)(2,1)} %get-tuple-element.499) | copy-start | bytes 7077892 | tf_op jit(solution)/shard_map/while
  207.5 8.0 %collective-permute-start = (bf16[4,2,64,256]{3,2,1,0:T(8,128)(2,1)S(1)}, bf16[4,2,64,256]{3,2,1,0:T(8,128)(2,1)S(1)}, u32[]{:S(2)}, u32[]{:S(2)}) collective-permute-start(bf16[4,2,64,256]{3,2,1,0:T(8,128)(2,1)S(1)} %get-tuple-element.471), channel_id=1, source_target_pairs={{8,0},{16,8},{24,16},{9,1},{17,9},{25,17},{10,2},{18,10},{26,18},{... | collective-permute-start | bytes 786440 | tf_op jit(solution)/shard_map/while/body/eval_jaxpr/ppermute | solution.py:23
  215.6 8.0 %collective-permute-start.2 = (bf16[4,2,64,256]{3,2,1,0:T(8,128)(2,1)S(1)}, bf16[4,2,64,256]{3,2,1,0:T(8,128)(2,1)S(1)}, u32[]{:S(2)}, u32[]{:S(2)}) collective-permute-start(bf16[4,2,64,256]{3,2,1,0:T(8,128)(2,1)S(1)} %maximum_select_fusion.3), channel_id=1, source_target_pairs={{0,1},{1,2},{2,3},{3,4},{4,5},{5,6},{6,7},{8,9},{9,10},{10,11},{11... | collective-permute-start | bytes 786440 | tf_op jit(solution)/shard_map/while/body/eval_jaxpr/ppermute | solution.py:14
  219.7 8.3 %collective-permute-start.1 = (bf16[4,2,64,256]{3,2,1,0:T(8,128)(2,1)S(1)}, bf16[4,2,64,256]{3,2,1,0:T(8,128)(2,1)S(1)}, u32[]{:S(2)}, u32[]{:S(2)}) collective-permute-start(bf16[4,2,64,256]{3,2,1,0:T(8,128)(2,1)S(1)} %maximum_select_fusion.3), channel_id=1, source_target_pairs={{1,0},{2,1},{3,2},{4,3},{5,4},{6,5},{7,6},{9,8},{10,9},{11,10},{12... | collective-permute-start | bytes 786440 | tf_op jit(solution)/shard_map/while/body/eval_jaxpr/ppermute | solution.py:15
  221.1 7.5 %copy-start.3 = (bf16[1,2,3,3,256,256]{5,4,3,2,1,0:T(8,128)(2,1)S(1)}, bf16[1,2,3,3,256,256]{5,4,3,2,1,0:T(8,128)(2,1)}, u32[]{:S(2)}) copy-start(bf16[1,2,3,3,256,256]{5,4,3,2,1,0:T(8,128)(2,1)} %get-tuple-element.499) | copy-start | bytes 7077892 | tf_op jit(solution)/shard_map/while
  239.4 129.9 %reduce-scatter.5.cloned.1.call-start = ((), (), s32[]{:S(2)}) async-start(), calls=%async_computation.3 | async-start | bytes 5308416 | tf_op jit(solution)/shard_map/reduce_scatter | solution.py:142
  (28 other events, 50.6 us)
Sparse Core Ops, SparseCore 0:
  239.5 29.6 reduce-scatter.2
  273.8 95.4 reduce-scatter.4
where the time goes:
time: 377 us; the launch traced here: 376 us
  waiting for transfers between devices  218 us (58%)
  starting transfers between devices  46.2 us (12%)
  local copies, waits for them, and re-layouts  43 us (11%)
  matrix products  19 us (5%)
  blocking collectives  16.3 us (4%)
  other arithmetic  15.1 us (4%)
  between operations  14.1 us (4%)
  loops' own time  4.01 us (1%)
    reduce_scatter x1, waiting for transfers between devices, local(): lax.psum_scatter(grads.reshape(term_rows, channels), 'rows', scatter_dime...  98.5 us
    ppermute x7, waiting for transfers between devices, from_behind(): return lax.ppermute(shard, axis, pairs)  42.2 us
    ppermute x7, waiting for transfers between devices, with_halo(): after = lax.ppermute(initial, axis, down)  30.9 us
    reduce_scatter x1, waiting for transfers between devices, local(): lax.psum_scatter(finished.astype(jnp.float32).astype(jnp.bfloat16), 'sec'...  29 us
    while x217, local copies, waits for them, and re-layouts  28.8 us
    ppermute x7, starting transfers between devices, with_halo(): before = lax.ppermute(last, axis, up)  28.1 us
    ppermute x7, waiting for transfers between devices, with_halo(): before = lax.ppermute(last, axis, up)  17.1 us
    conv_general_dilated x28, matrix products, conv_rows(): lax.conv_general_dilated(field[None], kernel, (1, 1), ((0, 0), (1, 1)), d...  12 us
  transfers between devices with their start and end apart: 23, of which 23 were waited for; matrix products, arithmetic and copies ran while one was open for 1% of the time, Pallas kernels for 0%

commit v1 on v0

v1 whole, which is shorter than its diff:
```python
import functools

import jax
import jax.numpy as jnp
from jax import lax
from jax.experimental import pallas as pl
from jax.experimental.pallas import tpu as pltpu
from jax.sharding import PartitionSpec as P

MESH = pl.DeviceIdType.MESH
F32 = jnp.float32
BF16 = jnp.bfloat16


def silu_slope(value):
    sig = jax.nn.sigmoid(value)
    return sig + value * sig * (1.0 - sig)


def shift_cols(value, by, width):
    pixels = value.shape[0]
    col = lax.rem(lax.broadcasted_iota(jnp.int32, value.shape, 0), width)
    rolled = pltpu.roll(value, by % pixels, axis=0)
    edge = 0 if by > 0 else width - 1
    return jnp.where(col == edge, 0.0, rolled)


def conv(field, kernel_ref, which, width, turned):
    pixels = field.shape[0] - 2 * width
    dims = (((1,), (1 if turned else 0,)), ((), ()))
    parts = []
    for b in range(3):
        total = None
        for a in range(3):
            tap = kernel_ref[which, 2 - a, 2 - b] if turned else kernel_ref[which, a, b]
            term = lax.dot_general(
                field[a * width : a * width + pixels], tap, dims, preferred_element_type=F32
            )
            total = term if total is None else total + term
        parts.append(total)
    return parts[1] + shift_cols(parts[0], 1, width) + shift_cols(parts[2], -1, width)


def add_grads(acc_ref, which, field, cotan, width):
    pixels, channels = cotan.shape
    wide = cotan.astype(F32)
    shifted = jnp.concatenate(
        [
            shift_cols(wide, -1, width).astype(BF16),
            cotan,
            shift_cols(wide, 1, width).astype(BF16),
        ],
        axis=1,
    )
    for a in range(3):
        term = lax.dot_general(
            field[a * width : a * width + pixels],
            shifted,
            (((0,), (0,)), ((), ())),
            preferred_element_type=F32,
        )
        for b in range(3):
            start = ((which * 3 + a) * 3 + b) * channels
            acc_ref[start : start + channels] += term[:, b * channels : (b + 1) * channels]


def body(
    S, N, scale,
    streams, cotangents, weights, out_streams, out_grads, out_weights,
    first, first_edge, state, made, edge_a, made_a, edge_b, made_b, result, acc, terms, got,
    first_send, st_send, st_recv, ea_send, ea_recv, eb_send, eb_recv,
    res_send, res_recv, rs_send, rs_recv,
):
    s, r = lax.axis_index("sec"), lax.axis_index("rows")
    M = S
    rows, width, channels = state.shape[2:]
    chunk = terms.shape[1]
    last_sec = s == S - 1
    below, above = lax.rem(r + 1, N), lax.rem(r + N - 1, N)
    has_above, has_below = r > 0, r < N - 1
    sides = ((0, above, has_above), (1, below, has_below))
    lower_sec = lax.rem(s + S - 1, S)

    def remote(src, dst, send, recv, sec, row):
        return pltpu.make_async_remote_copy(
            src_ref=src, dst_ref=dst, send_sem=send, recv_sem=recv,
            device_id=(sec, row), device_id_type=MESH,
        )

    barrier = pltpu.get_barrier_semaphore()
    for step in range(S):
        sec = lax.rem(s + step, S)
        if step > 0:
            pl.semaphore_signal(barrier, inc=1, device_id=(sec, r), device_id_type=MESH)
        for _, row, there in sides:
            if step > 0:
                @pl.when(there)
                def _(sec=sec, row=row):
                    pl.semaphore_signal(barrier, inc=1, device_id=(sec, row), device_id_type=MESH)
    for step in range(1, N):
        pl.semaphore_signal(
            barrier, inc=1, device_id=(s, lax.rem(r + step, N)), device_id_type=MESH
        )

    own = S - 1 - s
    first[0] = streams[0, 0]
    first[1] = cotangents[0, 1]
    first[2] = streams[0, 1]
    first[3] = cotangents[0, 0]
    for side in range(2):
        row = 0 if side == 0 else rows - 1
        first_edge[side, 0] = streams[0, 0, row]
        first_edge[side, 1] = cotangents[0, 1, row]

    @pl.when(last_sec)
    def _():
        state[0] = first[...]

    for side, _, there in sides:
        @pl.when(jnp.logical_not(there))
        def _(side=side):
            edge_a[:, side] = jnp.zeros(edge_a.shape[:1] + edge_a.shape[2:], BF16)
            edge_b[:, side] = jnp.zeros(edge_b.shape[:1] + edge_b.shape[2:], BF16)

    near = 1 + has_above.astype(jnp.int32) + has_below.astype(jnp.int32)
    pl.semaphore_wait(barrier, (S - 1) * near + N - 1)

    def first_edges(side, row):
        return remote(
            first_edge.at[side], edge_a.at[own, 1 - side],
            first_send.at[2 + side], ea_recv.at[own, 1 - side], S - 1, row,
        )

    def first_states(half):
        return remote(
            first.at[pl.ds(2 * half, 2)], state.at[own, pl.ds(2 * half, 2)],
            first_send.at[half], st_recv.at[own, half], S - 1, r,
        )

    for side, row, there in sides:
        @pl.when(there)
        def _(side=side, row=row):
            first_edges(side, row).start()

    @pl.when(jnp.logical_not(last_sec))
    def _():
        for half in range(2):
            first_states(half).start()

    acc[...] = jnp.zeros(acc.shape, F32)

    def state_copy(m, half):
        return remote(
            made.at[m, pl.ds(2 * half, 2)], state.at[m, pl.ds(2 * half, 2)],
            st_send.at[m, half], st_recv.at[m, half], lower_sec, r,
        )

    def result_copy(m, half):
        return remote(
            made.at[m, pl.ds(2 * half, 2)], result.at[pl.ds(2 * half, 2)],
            res_send.at[m, half], res_recv.at[half], S - 1 - m, r,
        )

    def edge_a_copy(m, side, row):
        return remote(
            made_a.at[m, side], edge_a.at[m, 1 - side],
            ea_send.at[m, side], ea_recv.at[m, 1 - side], lower_sec, row,
        )

    def edge_b_copy(m, side, row):
        return remote(
            made_b.at[m, side], edge_b.at[m, 1 - side],
            eb_send.at[m, side], eb_recv.at[m, 1 - side], s, row,
        )

    def send_half(m, half):
        @pl.when(s > 0)
        def _():
            state_copy(m, half).start()

        @pl.when((s == 0) & (m < M - 1))
        def _():
            result_copy(m, half).start()

    def term_copy(p):
        return remote(terms.at[p], got.at[r], rs_send.at[p], rs_recv.at[r], s, p)

    def send_terms(low, count):
        def one(i, carry):
            p = low + lax.rem(r + 1 + i, count)
            @pl.when(p != r)
            def _():
                start = pl.multiple_of(p * chunk, chunk)
                terms[p] = acc[pl.ds(start, chunk)].astype(terms.dtype)
                term_copy(p).start()
            return carry
        lax.fori_loop(0, count, one, 0)

    def flat(value):
        return value.reshape(-1, channels)

    def step(m, carry):
        for side, row, there in sides:
            @pl.when(there)
            def _(side=side, row=row):
                edge_a_copy(m, 1 - side, row).wait_recv()

        arrives = jnp.logical_not(last_sec & (m == 0))

        @pl.when(arrives)
        def _():
            state_copy(m, 0).wait_recv()
            state_copy(m, 1).wait_recv()

        y1 = flat(state[m, 0]).astype(F32)
        g2 = flat(state[m, 1])
        upper = jnp.concatenate([edge_a[m, 0, 0], flat(state[m, 0]), edge_a[m, 1, 0]], 0)
        act_g = jax.nn.silu(upper.astype(F32)).astype(BF16)
        g2_wide = jnp.concatenate([edge_a[m, 0, 1], g2, edge_a[m, 1, 1]], 0)
        x2 = (flat(state[m, 2]).astype(F32) - conv(act_g, weights, 1, width, False)).astype(BF16)
        carried = (
            flat(state[m, 3]).astype(F32)
            + conv(g2_wide, weights, 1, width, True) * silu_slope(y1)
        ).astype(BF16)
        made_b[m, 0, 0] = x2[:width]
        made_b[m, 0, 1] = carried[:width]
        made_b[m, 1, 0] = x2[-width:]
        made_b[m, 1, 1] = carried[-width:]
        for side, row, there in sides:
            @pl.when(there)
            def _(side=side, row=row):
                edge_b_copy(m, side, row).start()
        made[m, 2] = x2.reshape(rows, width, channels)
        made[m, 3] = carried.reshape(rows, width, channels)
        send_half(m, 1)

        add_grads(acc, 1, act_g, g2, width)

        @pl.when(m == M - 1)
        def _():
            send_terms(N // 2, N - N // 2)

        for side, row, there in sides:
            @pl.when(there)
            def _(side=side, row=row):
                edge_b_copy(m, 1 - side, row).wait_recv()
        lower = jnp.concatenate([edge_b[m, 0, 0], x2, edge_b[m, 1, 0]], 0)
        act_f = jax.nn.silu(lower.astype(F32)).astype(BF16)
        carried_wide = jnp.concatenate([edge_b[m, 0, 1], carried, edge_b[m, 1, 1]], 0)
        x1 = (y1 - conv(act_f, weights, 0, width, False)).astype(BF16)
        gx2 = (
            g2.astype(F32)
            + conv(carried_wide, weights, 0, width, True) * silu_slope(x2.astype(F32))
        ).astype(BF16)
        made_a[m, 0, 0] = x1[:width]
        made_a[m, 0, 1] = gx2[:width]
        made_a[m, 1, 0] = x1[-width:]
        made_a[m, 1, 1] = gx2[-width:]
        for side, row, there in sides:
            @pl.when(there & (s > 0))
            def _(side=side, row=row):
                edge_a_copy(m, side, row).start()
        made[m, 0] = x1.reshape(rows, width, channels)
        made[m, 1] = gx2.reshape(rows, width, channels)
        send_half(m, 0)

        add_grads(acc, 0, act_f, carried, width)
        return carry

    lax.fori_loop(0, M, step, 0)
    send_terms(0, N // 2)

    def deliver(source):
        out_streams[0, 0] = source[0]
        out_grads[0, 1] = source[1]
        out_streams[0, 1] = source[2]
        out_grads[0, 0] = source[3]

    @pl.when(s == 0)
    def _():
        deliver(made[M - 1])

    @pl.when(s > 0)
    def _():
        result_copy(0, 0).wait_recv()
        result_copy(0, 1).wait_recv()
        deliver(result[...])

    out_weights[0] = acc[pl.ds(pl.multiple_of(r * chunk, chunk), chunk)] * scale

    def gather(i, carry):
        p = lax.rem(r + i, N)
        remote(terms.at[p], got.at[p], rs_send.at[p], rs_recv.at[p], s, p).wait_recv()
        out_weights[0] += got[p].astype(F32) * scale
        return carry

    lax.fori_loop(1, N, gather, 0)

    for side, row, there in sides:
        @pl.when(there)
        def _(side=side, row=row):
            first_edges(side, row).wait_send()

    @pl.when(jnp.logical_not(last_sec))
    def _():
        for half in range(2):
            first_states(half).wait_send()

    def drain(m, carry):
        for side, row, there in sides:
            @pl.when(there)
            def _(side=side, row=row):
                edge_b_copy(m, side, row).wait_send()

            @pl.when(there & (s > 0))
            def _(side=side, row=row):
                edge_a_copy(m, side, row).wait_send()

        for half in range(2):
            @pl.when(s > 0)
            def _(half=half):
                state_copy(m, half).wait_send()

            @pl.when((s == 0) & (m < M - 1))
            def _(half=half):
                result_copy(m, half).wait_send()
        return carry

    lax.fori_loop(0, M, drain, 0)

    def drain_terms(i, carry):
        term_copy(lax.rem(r + i, N)).wait_send()
        return carry

    lax.fori_loop(1, N, drain_terms, 0)


def local(S, N, streams, cotangents, weights):
    mine, _, rows, width, channels = streams.shape
    layers = weights.shape[1]
    assert mine == 1 and layers == 1 and N % 2 == 0
    M = S
    scale = (M * rows * N * width) ** -0.5
    total = 18 * channels
    chunk = total // N
    sent = BF16 if chunk % 16 == 0 else F32
    dma = pltpu.SemaphoreType.DMA
    vmem = pl.BlockSpec(memory_space=pltpu.VMEM)
    shard = (rows, width, channels)
    edge = (2, 2, width, channels)
    return pl.pallas_call(
        functools.partial(body, S, N, scale),
        out_shape=(
            jax.ShapeDtypeStruct(streams.shape, BF16),
            jax.ShapeDtypeStruct(streams.shape, BF16),
            jax.ShapeDtypeStruct((1, chunk, channels), F32),
        ),
        in_specs=[vmem] * 3,
        out_specs=(vmem,) * 3,
        scratch_shapes=[
            pltpu.VMEM((4,) + shard, BF16),
            pltpu.VMEM(edge, BF16),
            pltpu.VMEM((M, 4) + shard, BF16),
            pltpu.VMEM((M, 4) + shard, BF16),
            pltpu.VMEM((M,) + edge, BF16),
            pltpu.VMEM((M,) + edge, BF16),
            pltpu.VMEM((M,) + edge, BF16),
            pltpu.VMEM((M,) + edge, BF16),
            pltpu.VMEM((4,) + shard, BF16),
            pltpu.VMEM((total, channels), F32),
            pltpu.VMEM((N, chunk, channels), sent),
            pltpu.VMEM((N, chunk, channels), sent),
            dma((4,)),
            dma((M, 2)), dma((M, 2)), dma((M, 2)), dma((M, 2)), dma((M, 2)), dma((M, 2)),
            dma((M, 2)), dma((2,)), dma((N,)), dma((N,)),
        ],
        compiler_params=pltpu.CompilerParams(
            collective_id=0, has_side_effects=True, vmem_limit_bytes=40 * 1024 * 1024
        ),
        cost_estimate=pl.CostEstimate(
            flops=M * 108 * rows * width * channels * channels,
            bytes_accessed=weights.size * 2,
            transcendentals=0,
        ),
    )(streams, cotangents, weights[0, 0])


def solution(mesh):
    placed = (
        P("sec", None, "rows", None, None),
        P("sec", None, "rows", None, None),
        P("sec", None, None, None, None, None, None),
    )
    return jax.shard_map(
        functools.partial(local, mesh.shape["sec"], mesh.shape["rows"]),
        mesh=mesh,
        in_specs=placed,
        out_specs=(
            P("sec", None, "rows", None, None),
            P("sec", None, "rows", None, None),
            P("sec", "rows", None),
        ),
        check_vma=False,
    )
```

time: 377 us -> 159 us (0.42)
  waiting for transfers between devices: 218 us -> 0 us
  Pallas kernels: 0 us -> 153 us
  starting transfers between devices: 46.2 us -> 0 us
  local copies, waits for them, and re-layouts: 43 us -> 5.59 us
  matrix products: 19 us -> 0 us
  blocking collectives: 16.3 us -> 0 us
  other arithmetic: 15.1 us -> 0 us
  between operations: 14.1 us -> 0.65 us
  loops' own time: 4.01 us -> 0 us
    pallas_call x0 -> x1, Pallas kernels: none -> 153 us  [local(): pl.pallas_call(functools.partial(body, S, N, scale), out_shape=(jax.Shape...]
    reduce_scatter x2 -> x0, waiting for transfers between devices: 128 us -> none  [the longest x1 98.5 us: local(): lax.psum_scatter(grads.reshape(term_rows, channels), 'rows', scatter_dime...]
    ppermute x21 -> x0, waiting for transfers between devices: 90.2 us -> none  [the longest x7 42.2 us: from_behind(): return lax.ppermute(shard, axis, pairs)]
    ppermute x21 -> x0, starting transfers between devices: 46.1 us -> none  [the longest x7 28.1 us: with_halo(): before = lax.ppermute(last, axis, up)]
    while x217 -> x0, local copies, waits for them, and re-layouts: 28.8 us -> none
    all_gather x2 -> x0, blocking collectives: 16.3 us -> none  [the longest x1 8.83 us: local(): lax.all_gather(streams, 'sec', axis=0, tiled=True)]
    conv_general_dilated x28 -> x0, matrix products: 12 us -> none  [conv_rows(): lax.conv_general_dilated(field[None], kernel, (1, 1), ((0, 0), (1, 1)), d...]
    dot_general x14 -> x0, matrix products: 6.94 us -> none  [tap_grads(): lax.dot_general(patches, cotan, (((1, 2), (0, 1)), ((), ())), preferred_e...]
  transfers between devices with their start and end apart: 23 -> 0, of which waited for: 23 -> 0; matrix products, arithmetic and copies ran while one was open for 1% -> 0% of each run, Pallas kernels for 0% -> 0%
where the time goes in v1:
time: 159 us
  Pallas kernels  153 us (96%)
  local copies, waits for them, and re-layouts  5.59 us (4%)
    pallas_call x1, Pallas kernels, local(): pl.pallas_call(functools.partial(body, S, N, scale), out_shape=(jax.Shape...  153 us
    unnamed x9, local copies, waits for them, and re-layouts  5.59 us

profile of v1, /device:TPU:0, one launch (start us, length us, event | category | flops | bytes accessed | tf_op | source)
XLA Modules:
  0.0 159.3 jit_solution(14306197992291346673)
XLA Ops:
  0.6 0.0 copy-start
  0.6 1.7 %copy-done = bf16[1,1,2,3,3,256,256]{6,5,4,3,2,1,0:T(8,128)(2,1)S(1)} copy-done((bf16[1,1,2,3,3,256,256]{6,5,4,3,2,1,0:T(8,128)(2,1)S(1)}, bf16[1,1,2,3,3,256,256]{6,5,4,3,2,1,0:T(8,128)(2,1)}, u32[]{:S(2)}) %copy-start) | copy-done | bytes 2359320
  2.3 0.0 copy-start.1
  2.3 0.9 copy-done.1
  3.2 0.0 copy-start.2
  3.2 0.9 copy-done.2
  4.1 153.1 %shard_map.58 = (bf16[1,2,2,64,256]{4,3,2,1,0:T(8,128)(2,1)S(1)}, bf16[1,2,2,64,256]{4,3,2,1,0:T(8,128)(2,1)S(1)}, f32[1,576,256]{2,1,0:T(8,128)S(1)}) custom-call(bf16[1,2,2,64,256]{4,3,2,1,0:T(8,128)(2,1)S(1)} %copy-done.1, bf16[1,2,2,64,256]{4,3,2,1,0:T(8,128)(2,1)S(1)} %copy-done.2, bf16[2,3,3,256,256]{4,3,2,1,0:T(8,128)(2,1)S(1)} %bitcast.1), custom_call_target="tpu_custom_call" | custom-call | flops 3623878656 | bytes 2359296 | tf_op jit(solution)/shard_map/pallas_call | solution.py:351
  157.2 0.7 copy.9
  157.8 0.7 copy.10
  158.5 0.8 copy.11
Async XLA Ops:
  0.6 1.7 %copy-start = (bf16[1,1,2,3,3,256,256]{6,5,4,3,2,1,0:T(8,128)(2,1)S(1)}, bf16[1,1,2,3,3,256,256]{6,5,4,3,2,1,0:T(8,128)(2,1)}, u32[]{:S(2)}) copy-start(bf16[1,1,2,3,3,256,256]{6,5,4,3,2,1,0:T(8,128)(2,1)} %param.5) | copy-start | bytes 7077892
  2.3 0.9 copy-start.1
  3.2 0.9 copy-start.2

commit v2 on v1

v2 whole, which is shorter than its diff:
```python
import functools

import jax
import jax.numpy as jnp
from jax import lax
from jax.experimental import pallas as pl
from jax.experimental.pallas import tpu as pltpu
from jax.sharding import PartitionSpec as P

MESH = pl.DeviceIdType.MESH
F32 = jnp.float32
BF16 = jnp.bfloat16


def silu_slope(value):
    sig = jax.nn.sigmoid(value)
    return sig + value * sig * (1.0 - sig)


def shift_cols(value, by, width):
    pixels = value.shape[0]
    col = lax.rem(lax.broadcasted_iota(jnp.int32, value.shape, 0), width)
    rolled = pltpu.roll(value, by % pixels, axis=0)
    edge = 0 if by > 0 else width - 1
    return jnp.where(col == edge, 0.0, rolled)


def conv(field, kernel_ref, which, width, turned):
    pixels = field.shape[0] - 2 * width
    dims = (((1,), (1 if turned else 0,)), ((), ()))
    parts = []
    for b in range(3):
        total = None
        for a in range(3):
            tap = kernel_ref[which, 2 - a, 2 - b] if turned else kernel_ref[which, a, b]
            term = lax.dot_general(
                field[a * width : a * width + pixels], tap, dims, preferred_element_type=F32
            )
            total = term if total is None else total + term
        parts.append(total)
    return parts[1] + shift_cols(parts[0], 1, width) + shift_cols(parts[2], -1, width)


def add_grads(acc_ref, which, field, cotan, width):
    pixels, channels = cotan.shape
    wide = cotan.astype(F32)
    shifted = jnp.concatenate(
        [
            shift_cols(wide, -1, width).astype(BF16),
            cotan,
            shift_cols(wide, 1, width).astype(BF16),
        ],
        axis=1,
    )
    for a in range(3):
        term = lax.dot_general(
            field[a * width : a * width + pixels],
            shifted,
            (((0,), (0,)), ((), ())),
            preferred_element_type=F32,
        )
        for b in range(3):
            start = ((which * 3 + a) * 3 + b) * channels
            acc_ref[start : start + channels] += term[:, b * channels : (b + 1) * channels]


def body(
    S, N, scale,
    streams, cotangents, weights_in, out_streams, out_grads, out_weights,
    weights, first, state, made, edge_a, edge_b, result, acc, terms, mid, sums, got,
    in_sem, w_sem, first_send, fedge_send, st_send, st_recv, ea_send, ea_recv, eb_send, eb_recv,
    res_send, res_recv, pair_send, pair_recv, rs_send, rs_recv,
):
    s, r = lax.axis_index("sec"), lax.axis_index("rows")
    M = S
    rows, width, channels = state.shape[2:]
    chunk = terms.shape[1]
    last_sec = s == S - 1
    below, above = lax.rem(r + 1, N), lax.rem(r + N - 1, N)
    has_above, has_below = r > 0, r < N - 1
    sides = ((0, above, has_above), (1, below, has_below))
    edge_row = (0, rows - 1)
    lower_sec = lax.rem(s + S - 1, S)
    half, group = lax.rem(r, 2), r // 2
    groups = N // 2
    partner = 2 * group + 1 - half

    def remote(src, dst, send, recv, sec, row):
        return pltpu.make_async_remote_copy(
            src_ref=src, dst_ref=dst, send_sem=send, recv_sem=recv,
            device_id=(sec, row), device_id_type=MESH,
        )

    own = S - 1 - s
    sources = (streams.at[0, 0], cotangents.at[0, 1], streams.at[0, 1], cotangents.at[0, 0])
    loads = [pltpu.make_async_copy(src, first.at[i], in_sem.at[i]) for i, src in enumerate(sources)]
    for load in loads:
        load.start()
    kernel_loads = [
        pltpu.make_async_copy(weights_in.at[0, 0, i], weights.at[i], w_sem.at[i]) for i in (1, 0)
    ]
    for load in kernel_loads:
        load.start()

    barrier = pltpu.get_barrier_semaphore()
    for step in range(S):
        sec = lax.rem(s + step, S)
        if step > 0:
            pl.semaphore_signal(barrier, inc=1, device_id=(sec, r), device_id_type=MESH)
        for _, row, there in sides:
            if step > 0:
                @pl.when(there)
                def _(sec=sec, row=row):
                    pl.semaphore_signal(barrier, inc=1, device_id=(sec, row), device_id_type=MESH)
    for step in range(1, N):
        pl.semaphore_signal(
            barrier, inc=1, device_id=(s, lax.rem(r + step, N)), device_id_type=MESH
        )

    for side, _, there in sides:
        @pl.when(jnp.logical_not(there))
        def _(side=side):
            edge_a[:, side] = jnp.zeros(edge_a.shape[:1] + edge_a.shape[2:], BF16)
            edge_b[:, side] = jnp.zeros(edge_b.shape[:1] + edge_b.shape[2:], BF16)

    for load in loads:
        load.wait()

    @pl.when(last_sec)
    def _():
        state[0] = first[...]

    near = 1 + has_above.astype(jnp.int32) + has_below.astype(jnp.int32)
    pl.semaphore_wait(barrier, (S - 1) * near + N - 1)

    def first_edge(i, side, row):
        return remote(
            first.at[i, edge_row[side]], edge_a.at[own, 1 - side, i],
            fedge_send.at[side, i], ea_recv.at[own, 2 * (1 - side) + i], S - 1, row,
        )

    def first_state(i):
        return remote(
            first.at[i], state.at[own, i], first_send.at[i], st_recv.at[own, i], S - 1, r,
        )

    for i in range(2):
        for side, row, there in sides:
            @pl.when(there)
            def _(i=i, side=side, row=row):
                first_edge(i, side, row).start()

    @pl.when(jnp.logical_not(last_sec))
    def _():
        for i in range(4):
            first_state(i).start()

    acc[...] = jnp.zeros(acc.shape, F32)
    for load in kernel_loads:
        load.wait()

    def state_copy(m, i):
        return remote(
            made.at[m, i], state.at[m, i], st_send.at[m, i], st_recv.at[m, i], lower_sec, r,
        )

    def result_copy(m, i):
        return remote(
            made.at[m, i], result.at[i], res_send.at[m, i], res_recv.at[i], S - 1 - m, r,
        )

    def edge_a_copy(m, i, side, row):
        return remote(
            made.at[m, i, edge_row[side]], edge_a.at[m, 1 - side, i],
            ea_send.at[m, 2 * side + i], ea_recv.at[m, 2 * (1 - side) + i], lower_sec, row,
        )

    def edge_b_copy(m, i, side, row):
        return remote(
            made.at[m, 2 + i, edge_row[side]], edge_b.at[m, 1 - side, i],
            eb_send.at[m, 2 * side + i], eb_recv.at[m, 2 * (1 - side) + i], s, row,
        )

    def send_on(m, i):
        @pl.when(s > 0)
        def _():
            state_copy(m, i).start()

        @pl.when((s == 0) & (m < M - 1))
        def _():
            result_copy(m, i).start()

    def rows_of(p):
        return pl.ds(pl.multiple_of(p * chunk, chunk), chunk)

    def pair_copy(k):
        return remote(terms.at[k], mid.at[k], pair_send.at[k], pair_recv.at[k], s, partner)

    def sum_copy(k):
        return remote(
            sums.at[k], got.at[group], rs_send.at[k], rs_recv.at[group], s, 2 * k + half
        )

    def send_pairs(low, count):
        def one(i, carry):
            k = low + lax.rem(group + 1 + i, count)
            terms[k] = acc[rows_of(2 * k + 1 - half)].astype(terms.dtype)
            pair_copy(k).start()
            return carry
        lax.fori_loop(0, count, one, 0)

    def send_sums(low, count):
        def one(i, carry):
            k = low + lax.rem(group + 1 + i, count)
            pair_copy(k).wait_recv()
            total = acc[rows_of(2 * k + half)] + mid[k].astype(F32)

            @pl.when(k == group)
            def _():
                out_weights[0] = total

            @pl.when(k != group)
            def _():
                sums[k] = total.astype(sums.dtype)
                sum_copy(k).start()
            return carry
        lax.fori_loop(0, count, one, 0)

    def flat(value):
        return value.reshape(-1, channels)

    def step(m, carry):
        arrives = jnp.logical_not(last_sec & (m == 0))

        def await_state(i):
            @pl.when(arrives)
            def _():
                state_copy(m, i).wait_recv()

        def await_edges(copy, i):
            for side, row, there in sides:
                @pl.when(there)
                def _(side=side, row=row):
                    copy(m, i, 1 - side, row).wait_recv()

        def send_edges(copy, i, ok=True):
            for side, row, there in sides:
                @pl.when(there & ok)
                def _(side=side, row=row):
                    copy(m, i, side, row).start()

        def grads_g():
            add_grads(acc, 1, act_g, g2, width)

        await_edges(edge_a_copy, 0)
        await_state(0)
        y1 = flat(state[m, 0])
        upper = jnp.concatenate([edge_a[m, 0, 0], y1, edge_a[m, 1, 0]], 0)
        act_g = jax.nn.silu(upper.astype(F32)).astype(BF16)
        moved = conv(act_g, weights, 1, width, False)
        await_state(2)
        x2 = (flat(state[m, 2]).astype(F32) - moved).astype(BF16)
        made[m, 2] = x2.reshape(rows, width, channels)
        send_edges(edge_b_copy, 0)
        send_on(m, 2)

        await_edges(edge_a_copy, 1)
        await_state(1)
        g2 = flat(state[m, 1])
        g2_wide = jnp.concatenate([edge_a[m, 0, 1], g2, edge_a[m, 1, 1]], 0)
        moved = conv(g2_wide, weights, 1, width, True) * silu_slope(y1.astype(F32))
        await_state(3)
        carried = (flat(state[m, 3]).astype(F32) + moved).astype(BF16)
        made[m, 3] = carried.reshape(rows, width, channels)
        send_edges(edge_b_copy, 1)
        send_on(m, 3)

        @pl.when(m == M - 1)
        def _():
            grads_g()
            send_pairs(groups // 2, groups - groups // 2)

        await_edges(edge_b_copy, 0)
        lower = jnp.concatenate([edge_b[m, 0, 0], x2, edge_b[m, 1, 0]], 0)
        act_f = jax.nn.silu(lower.astype(F32)).astype(BF16)
        x1 = (y1.astype(F32) - conv(act_f, weights, 0, width, False)).astype(BF16)
        made[m, 0] = x1.reshape(rows, width, channels)
        send_edges(edge_a_copy, 0, s > 0)
        send_on(m, 0)

        await_edges(edge_b_copy, 1)
        carried_wide = jnp.concatenate([edge_b[m, 0, 1], carried, edge_b[m, 1, 1]], 0)
        moved = conv(carried_wide, weights, 0, width, True) * silu_slope(x2.astype(F32))
        made[m, 1] = (g2.astype(F32) + moved).astype(BF16).reshape(rows, width, channels)
        send_edges(edge_a_copy, 1, s > 0)
        send_on(m, 1)

        @pl.when(m < M - 1)
        def _():
            grads_g()

        add_grads(acc, 0, act_f, carried, width)
        return carry

    lax.fori_loop(0, M, step, 0)
    send_pairs(0, groups // 2)
    send_sums(groups // 2, groups - groups // 2)
    send_sums(0, groups // 2)

    def deliver(source):
        out_streams[0, 0] = source[0]
        out_grads[0, 1] = source[1]
        out_streams[0, 1] = source[2]
        out_grads[0, 0] = source[3]

    @pl.when(s == 0)
    def _():
        deliver(made[M - 1])

    @pl.when(s > 0)
    def _():
        for i in range(4):
            result_copy(0, i).wait_recv()
        deliver(result[...])

    for side, row, there in sides:
        @pl.when(there)
        def _(side=side, row=row):
            for i in range(2):
                first_edge(i, side, row).wait_send()

    @pl.when(jnp.logical_not(last_sec))
    def _():
        for i in range(4):
            first_state(i).wait_send()

    def drain(m, carry):
        for side, row, there in sides:
            @pl.when(there)
            def _(side=side, row=row):
                for i in range(2):
                    edge_b_copy(m, i, side, row).wait_send()

            @pl.when(there & (s > 0))
            def _(side=side, row=row):
                for i in range(2):
                    edge_a_copy(m, i, side, row).wait_send()

        @pl.when(s > 0)
        def _():
            for i in range(4):
                state_copy(m, i).wait_send()

        @pl.when((s == 0) & (m < M - 1))
        def _():
            for i in range(4):
                result_copy(m, i).wait_send()
        return carry

    lax.fori_loop(0, M, drain, 0)

    def gather(i, carry):
        k = lax.rem(group + groups - i, groups)
        remote(
            sums.at[k], got.at[k], rs_send.at[k], rs_recv.at[k], s, 2 * k + half
        ).wait_recv()
        out_weights[0] += got[k].astype(F32)
        return carry

    lax.fori_loop(1, groups, gather, 0)
    out_weights[...] = out_weights[...] * scale

    def drain_terms(k, carry):
        pair_copy(k).wait_send()

        @pl.when(k != group)
        def _():
            sum_copy(k).wait_send()
        return carry

    lax.fori_loop(0, groups, drain_terms, 0)


def local(S, N, streams, cotangents, weights):
    mine, _, rows, width, channels = streams.shape
    layers = weights.shape[1]
    assert mine == 1 and layers == 1 and N % 2 == 0
    M = S
    scale = (M * rows * N * width) ** -0.5
    total = 18 * channels
    chunk = total // N
    sent = BF16 if chunk % 16 == 0 else F32
    dma = pltpu.SemaphoreType.DMA
    vmem = pl.BlockSpec(memory_space=pltpu.VMEM)
    shard = (rows, width, channels)
    edge = (2, 2, width, channels)
    return pl.pallas_call(
        functools.partial(body, S, N, scale),
        out_shape=(
            jax.ShapeDtypeStruct(streams.shape, BF16),
            jax.ShapeDtypeStruct(streams.shape, BF16),
            jax.ShapeDtypeStruct((1, chunk, channels), F32),
        ),
        in_specs=[pl.BlockSpec(memory_space=pl.ANY)] * 3,
        out_specs=(vmem,) * 3,
        scratch_shapes=[
            pltpu.VMEM(weights.shape[2:], BF16),
            pltpu.VMEM((4,) + shard, BF16),
            pltpu.VMEM((M, 4) + shard, BF16),
            pltpu.VMEM((M, 4) + shard, BF16),
            pltpu.VMEM((M,) + edge, BF16),
            pltpu.VMEM((M,) + edge, BF16),
            pltpu.VMEM((4,) + shard, BF16),
            pltpu.VMEM((total, channels), F32),
            pltpu.VMEM((N // 2, chunk, channels), sent),
            pltpu.VMEM((N // 2, chunk, channels), sent),
            pltpu.VMEM((N // 2, chunk, channels), sent),
            pltpu.VMEM((N // 2, chunk, channels), sent),
            dma((4,)), dma((2,)), dma((4,)), dma((2, 2)),
            dma((M, 4)), dma((M, 4)), dma((M, 4)), dma((M, 4)), dma((M, 4)), dma((M, 4)),
            dma((M, 4)), dma((4,)),
            dma((N // 2,)), dma((N // 2,)), dma((N // 2,)), dma((N // 2,)),
        ],
        compiler_params=pltpu.CompilerParams(
            collective_id=0, has_side_effects=True, vmem_limit_bytes=40 * 1024 * 1024
        ),
        cost_estimate=pl.CostEstimate(
            flops=M * 108 * rows * width * channels * channels,
            bytes_accessed=weights.size * 2,
            transcendentals=0,
        ),
    )(streams, cotangents, weights)


def solution(mesh):
    placed = (
        P("sec", None, "rows", None, None),
        P("sec", None, "rows", None, None),
        P("sec", None, None, None, None, None, None),
    )
    return jax.shard_map(
        functools.partial(local, mesh.shape["sec"], mesh.shape["rows"]),
        mesh=mesh,
        in_specs=placed,
        out_specs=(
            P("sec", None, "rows", None, None),
            P("sec", None, "rows", None, None),
            P("sec", "rows", None),
        ),
        check_vma=False,
    )
```

time: 159 us -> 108 us (0.68)
  Pallas kernels: 153 us -> 101 us
    pallas_call x1, Pallas kernels: 153 us -> 101 us  [local(): pl.pallas_call(functools.partial(body, S, N, scale), out_shape=(jax.Shape...]
where the time goes in v2:
time: 108 us
  Pallas kernels  101 us (94%)
  local copies, waits for them, and re-layouts  5.59 us (5%)
    pallas_call x1, Pallas kernels, local(): pl.pallas_call(functools.partial(body, S, N, scale), out_shape=(jax.Shape...  101 us
    unnamed x9, local copies, waits for them, and re-layouts  5.59 us

profile of v2, /device:TPU:0, one launch (start us, length us, event | category | flops | bytes accessed | tf_op | source)
XLA Modules:
  0.0 107.6 jit_solution(14850311917396563081)
XLA Ops:
  0.6 0.0 copy-start
  0.6 1.7 %copy-done = bf16[1,1,2,3,3,256,256]{6,5,4,3,2,1,0:T(8,128)(2,1)S(1)} copy-done((bf16[1,1,2,3,3,256,256]{6,5,4,3,2,1,0:T(8,128)(2,1)S(1)}, bf16[1,1,2,3,3,256,256]{6,5,4,3,2,1,0:T(8,128)(2,1)}, u32[]{:S(2)}) %copy-start) | copy-done | bytes 2359320
  2.3 0.0 copy-start.1
  2.3 0.9 copy-done.1
  3.2 0.0 copy-start.2
  3.2 0.9 copy-done.2
  4.1 101.3 %shard_map.58 = (bf16[1,2,2,64,256]{4,3,2,1,0:T(8,128)(2,1)S(1)}, bf16[1,2,2,64,256]{4,3,2,1,0:T(8,128)(2,1)S(1)}, f32[1,576,256]{2,1,0:T(8,128)S(1)}) custom-call(bf16[1,2,2,64,256]{4,3,2,1,0:T(8,128)(2,1)S(1)} %copy-done.1, bf16[1,2,2,64,256]{4,3,2,1,0:T(8,128)(2,1)S(1)} %copy-done.2, bf16[1,1,2,3,3,256,256]{6,5,4,3,2,1,0:T(8,128)(2,1)S(1)} %copy-done), custom_call_target="tpu_custom_call" | custom-call | flops 3623878656 | bytes 2359296 | tf_op jit(solution)/shard_map/pallas_call | solution.py:397
  105.4 0.7 copy.9
  106.1 0.7 copy.10
  106.8 0.8 copy.11
Async XLA Ops:
  0.6 1.7 %copy-start = (bf16[1,1,2,3,3,256,256]{6,5,4,3,2,1,0:T(8,128)(2,1)S(1)}, bf16[1,1,2,3,3,256,256]{6,5,4,3,2,1,0:T(8,128)(2,1)}, u32[]{:S(2)}) copy-start(bf16[1,1,2,3,3,256,256]{6,5,4,3,2,1,0:T(8,128)(2,1)} %weights_in.1) | copy-start | bytes 7077892
  2.3 0.9 copy-start.1
  3.2 0.9 copy-start.2

commit v3 on v2

--- a/solution.py
+++ b/solution.py
@@ -25,20 +25,14 @@
     return jnp.where(col == edge, 0.0, rolled)
 
 
-def conv(field, kernel_ref, which, width, turned):
-    pixels = field.shape[0] - 2 * width
-    dims = (((1,), (1 if turned else 0,)), ((), ()))
-    parts = []
-    for b in range(3):
-        total = None
-        for a in range(3):
-            tap = kernel_ref[which, 2 - a, 2 - b] if turned else kernel_ref[which, a, b]
-            term = lax.dot_general(
-                field[a * width : a * width + pixels], tap, dims, preferred_element_type=F32
-            )
-            total = term if total is None else total + term
-        parts.append(total)
-    return parts[1] + shift_cols(parts[0], 1, width) + shift_cols(parts[2], -1, width)
+def conv(field, kernel, width, turned):
+    pixels, channels = field.shape[0] - 2 * width, field.shape[1]
+    stacked = jnp.concatenate([field[a * width : a * width + pixels] for a in range(3)], 1)
+    wide = lax.dot_general(
+        stacked, kernel, (((1,), (1 if turned else 0,)), ((), ())), preferred_element_type=F32
+    )
+    left, centre, right = (wide[:, b * channels : (b + 1) * channels] for b in range(3))
+    return centre + shift_cols(left, 1, width) + shift_cols(right, -1, width)
 
 
 def add_grads(acc_ref, which, field, cotan, width):
@@ -67,7 +61,7 @@
 def body(
     S, N, scale,
     streams, cotangents, weights_in, out_streams, out_grads, out_weights,
-    weights, first, state, made, edge_a, edge_b, result, acc, terms, mid, sums, got,
+    taps, turned, first, state, made, edge_a, edge_b, result, acc, terms, mid, sums, got,
     in_sem, w_sem, first_send, fedge_send, st_send, st_recv, ea_send, ea_recv, eb_send, eb_recv,
     res_send, res_recv, pair_send, pair_recv, rs_send, rs_recv,
 ):
@@ -96,11 +90,18 @@
     loads = [pltpu.make_async_copy(src, first.at[i], in_sem.at[i]) for i, src in enumerate(sources)]
     for load in loads:
         load.start()
-    kernel_loads = [
-        pltpu.make_async_copy(weights_in.at[0, 0, i], weights.at[i], w_sem.at[i]) for i in (1, 0)
-    ]
-    for load in kernel_loads:
-        load.start()
+    for which in (1, 0):
+        for a in range(3):
+            for b in range(3):
+                rows_a, cols_b = pl.ds(a * channels, channels), pl.ds(b * channels, channels)
+                pltpu.make_async_copy(
+                    weights_in.at[0, 0, which, a, b], taps.at[which, rows_a, cols_b],
+                    w_sem.at[0, which],
+                ).start()
+                pltpu.make_async_copy(
+                    weights_in.at[0, 0, which, 2 - a, 2 - b], turned.at[which, cols_b, rows_a],
+                    w_sem.at[1, which],
+                ).start()
 
     barrier = pltpu.get_barrier_semaphore()
     for step in range(S):
@@ -156,8 +157,9 @@
             first_state(i).start()
 
     acc[...] = jnp.zeros(acc.shape, F32)
-    for load in kernel_loads:
-        load.wait()
+    for i, kept in enumerate((taps, turned)):
+        for which in range(2):
+            pltpu.make_async_copy(kept.at[which], kept.at[which], w_sem.at[i, which]).wait()
 
     def state_copy(m, i):
         return remote(
@@ -257,7 +259,7 @@
         y1 = flat(state[m, 0])
         upper = jnp.concatenate([edge_a[m, 0, 0], y1, edge_a[m, 1, 0]], 0)
         act_g = jax.nn.silu(upper.astype(F32)).astype(BF16)
-        moved = conv(act_g, weights, 1, width, False)
+        moved = conv(act_g, taps[1], width, False)
         await_state(2)
         x2 = (flat(state[m, 2]).astype(F32) - moved).astype(BF16)
         made[m, 2] = x2.reshape(rows, width, channels)
@@ -268,7 +270,7 @@
         await_state(1)
         g2 = flat(state[m, 1])
         g2_wide = jnp.concatenate([edge_a[m, 0, 1], g2, edge_a[m, 1, 1]], 0)
-        moved = conv(g2_wide, weights, 1, width, True) * silu_slope(y1.astype(F32))
+        moved = conv(g2_wide, turned[1], width, True) * silu_slope(y1.astype(F32))
         await_state(3)
         carried = (flat(state[m, 3]).astype(F32) + moved).astype(BF16)
         made[m, 3] = carried.reshape(rows, width, channels)
@@ -283,14 +285,14 @@
         await_edges(edge_b_copy, 0)
         lower = jnp.concatenate([edge_b[m, 0, 0], x2, edge_b[m, 1, 0]], 0)
         act_f = jax.nn.silu(lower.astype(F32)).astype(BF16)
-        x1 = (y1.astype(F32) - conv(act_f, weights, 0, width, False)).astype(BF16)
+        x1 = (y1.astype(F32) - conv(act_f, taps[0], width, False)).astype(BF16)
         made[m, 0] = x1.reshape(rows, width, channels)
         send_edges(edge_a_copy, 0, s > 0)
         send_on(m, 0)
 
         await_edges(edge_b_copy, 1)
         carried_wide = jnp.concatenate([edge_b[m, 0, 1], carried, edge_b[m, 1, 1]], 0)
-        moved = conv(carried_wide, weights, 0, width, True) * silu_slope(x2.astype(F32))
+        moved = conv(carried_wide, turned[0], width, True) * silu_slope(x2.astype(F32))
         made[m, 1] = (g2.astype(F32) + moved).astype(BF16).reshape(rows, width, channels)
         send_edges(edge_a_copy, 1, s > 0)
         send_on(m, 1)
@@ -401,10 +403,11 @@
             jax.ShapeDtypeStruct(streams.shape, BF16),
             jax.ShapeDtypeStruct((1, chunk, channels), F32),
         ),
-        in_specs=[pl.BlockSpec(memory_space=pl.ANY)] * 3,
+        in_specs=[pl.BlockSpec(memory_space=pltpu.HBM)] * 3,
         out_specs=(vmem,) * 3,
         scratch_shapes=[
-            pltpu.VMEM(weights.shape[2:], BF16),
+            pltpu.VMEM((2, 3 * channels, 3 * channels), BF16),
+            pltpu.VMEM((2, 3 * channels, 3 * channels), BF16),
             pltpu.VMEM((4,) + shard, BF16),
             pltpu.VMEM((M, 4) + shard, BF16),
             pltpu.VMEM((M, 4) + shard, BF16),
@@ -416,13 +419,13 @@
             pltpu.VMEM((N // 2, chunk, channels), sent),
             pltpu.VMEM((N // 2, chunk, channels), sent),
             pltpu.VMEM((N // 2, chunk, channels), sent),
-            dma((4,)), dma((2,)), dma((4,)), dma((2, 2)),
+            dma((4,)), dma((2, 2)), dma((4,)), dma((2, 2)),
             dma((M, 4)), dma((M, 4)), dma((M, 4)), dma((M, 4)), dma((M, 4)), dma((M, 4)),
             dma((M, 4)), dma((4,)),
             dma((N // 2,)), dma((N // 2,)), dma((N // 2,)), dma((N // 2,)),
         ],
         compiler_params=pltpu.CompilerParams(
-            collective_id=0, has_side_effects=True, vmem_limit_bytes=40 * 1024 * 1024
+            collective_id=0, has_side_effects=True, vmem_limit_bytes=64 * 1024 * 1024
         ),
         cost_estimate=pl.CostEstimate(
             flops=M * 108 * rows * width * channels * channels,

time: 108 us -> 106 us (0.981)
    unnamed x9 -> x3, local copies, waits for them, and re-layouts: 5.59 us -> 5.05 us
where the time goes in v3:
time: 106 us
  Pallas kernels  100 us (94%)
  local copies, waits for them, and re-layouts  5.05 us (5%)
    pallas_call x1, Pallas kernels, local(): pl.pallas_call(functools.partial(body, S, N, scale), out_shape=(jax.Shape...  100 us
    unnamed x3, local copies, waits for them, and re-layouts  5.05 us

profile of v3, /device:TPU:0, one launch (start us, length us, event | category | flops | bytes accessed | tf_op | source)
XLA Modules:
  0.0 106.0 jit_solution(1314733838458500007)
XLA Ops:
  0.6 100.3 %shard_map.58 = (bf16[1,2,2,64,256]{4,3,2,1,0:T(8,128)(2,1)}, bf16[1,2,2,64,256]{4,3,2,1,0:T(8,128)(2,1)}, f32[1,576,256]{2,1,0:T(8,128)}) custom-call(bf16[1,2,2,64,256]{4,3,2,1,0:T(8,128)(2,1)} %streams.1, bf16[1,2,2,64,256]{4,3,2,1,0:T(8,128)(2,1)} %cotangents.1, bf16[1,1,2,3,3,256,256]{6,5,4,3,2,1,0:T(8,128)(2,1)} %weights_in.1), custom_call_target="tpu_custom_call" | custom-call | flops 3623878656 | bytes 2359296 | tf_op jit(solution)/shard_map/pallas_call | solution.py:399
  101.0 1.6 %copy.9 = bf16[1,2,2,64,256]{4,3,2,1,0:T(8,128)(2,1)} copy(bf16[1,2,2,64,256]{4,3,2,1,0:T(8,128)(2,1)} %get-tuple-element.6) | data formatting | bytes 262144
  102.5 1.6 %copy.10 = bf16[1,2,2,64,256]{4,3,2,1,0:T(8,128)(2,1)} copy(bf16[1,2,2,64,256]{4,3,2,1,0:T(8,128)(2,1)} %get-tuple-element.7) | data formatting | bytes 262144
  104.1 1.9 %copy.11 = f32[1,576,256]{2,1,0:T(8,128)} copy(f32[1,576,256]{2,1,0:T(8,128)} %get-tuple-element.8) | data formatting | bytes 1179648

commit v4 on v3

--- a/solution.py
+++ b/solution.py
@@ -25,45 +25,46 @@
     return jnp.where(col == edge, 0.0, rolled)
 
 
-def conv(field, kernel, width, turned):
+def conv(field, kernel, width):
     pixels, channels = field.shape[0] - 2 * width, field.shape[1]
     stacked = jnp.concatenate([field[a * width : a * width + pixels] for a in range(3)], 1)
-    wide = lax.dot_general(
-        stacked, kernel, (((1,), (1 if turned else 0,)), ((), ())), preferred_element_type=F32
-    )
+    wide = jnp.dot(stacked, kernel, preferred_element_type=F32)
     left, centre, right = (wide[:, b * channels : (b + 1) * channels] for b in range(3))
     return centre + shift_cols(left, 1, width) + shift_cols(right, -1, width)
 
 
-def add_grads(acc_ref, which, field, cotan, width):
-    pixels, channels = cotan.shape
-    wide = cotan.astype(F32)
-    shifted = jnp.concatenate(
-        [
-            shift_cols(wide, -1, width).astype(BF16),
-            cotan,
-            shift_cols(wide, 1, width).astype(BF16),
-        ],
-        axis=1,
-    )
+def all_grads(acc_ref, which, fields, cotans, width):
+    pixels, channels = cotans[0].shape
+    shifted = []
+    for cotan in cotans:
+        wide = cotan.astype(F32)
+        shifted.append(
+            jnp.concatenate(
+                [
+                    shift_cols(wide, -1, width).astype(BF16),
+                    cotan,
+                    shift_cols(wide, 1, width).astype(BF16),
+                ],
+                axis=1,
+            )
+        )
+    shifted = jnp.concatenate(shifted, 0)
     for a in range(3):
+        stacked = jnp.concatenate([f[a * width : a * width + pixels] for f in fields], 0)
         term = lax.dot_general(
-            field[a * width : a * width + pixels],
-            shifted,
-            (((0,), (0,)), ((), ())),
-            preferred_element_type=F32,
+            stacked, shifted, (((0,), (0,)), ((), ())), preferred_element_type=F32
         )
         for b in range(3):
             start = ((which * 3 + a) * 3 + b) * channels
-            acc_ref[start : start + channels] += term[:, b * channels : (b + 1) * channels]
+            acc_ref[start : start + channels] = term[:, b * channels : (b + 1) * channels]
 
 
 def body(
     S, N, scale,
     streams, cotangents, weights_in, out_streams, out_grads, out_weights,
-    taps, turned, first, state, made, edge_a, edge_b, result, acc, terms, mid, sums, got,
+    taps, turned, first, state, made, edge_a, edge_b, keep_g, keep_f, result, acc, terms, mid, sums, got,
     in_sem, w_sem, first_send, fedge_send, st_send, st_recv, ea_send, ea_recv, eb_send, eb_recv,
-    res_send, res_recv, pair_send, pair_recv, rs_send, rs_recv,
+    res_send, res_recv, pair_send, pair_recv, rs_send, rs_recv, go,
 ):
     s, r = lax.axis_index("sec"), lax.axis_index("rows")
     M = S
@@ -96,11 +97,7 @@
                 rows_a, cols_b = pl.ds(a * channels, channels), pl.ds(b * channels, channels)
                 pltpu.make_async_copy(
                     weights_in.at[0, 0, which, a, b], taps.at[which, rows_a, cols_b],
-                    w_sem.at[0, which],
-                ).start()
-                pltpu.make_async_copy(
-                    weights_in.at[0, 0, which, 2 - a, 2 - b], turned.at[which, cols_b, rows_a],
-                    w_sem.at[1, which],
+                    w_sem.at[which],
                 ).start()
 
     barrier = pltpu.get_barrier_semaphore()
@@ -145,6 +142,10 @@
             first.at[i], state.at[own, i], first_send.at[i], st_recv.at[own, i], S - 1, r,
         )
 
+    @pl.when(own >= 2)
+    def _():
+        pl.semaphore_wait(go, 1)
+
     for i in range(2):
         for side, row, there in sides:
             @pl.when(there)
@@ -156,10 +157,17 @@
         for i in range(4):
             first_state(i).start()
 
-    acc[...] = jnp.zeros(acc.shape, F32)
-    for i, kept in enumerate((taps, turned)):
-        for which in range(2):
-            pltpu.make_async_copy(kept.at[which], kept.at[which], w_sem.at[i, which]).wait()
+    for which in (1, 0):
+        pltpu.make_async_copy(taps.at[which], taps.at[which], w_sem.at[which]).wait()
+        for a in range(3):
+            for b in range(3):
+                turned[which, a * channels : (a + 1) * channels, b * channels : (b + 1) * channels] = (
+                    taps[
+                        which,
+                        (2 - a) * channels : (3 - a) * channels,
+                        (2 - b) * channels : (3 - b) * channels,
+                    ].T
+                )
 
     def state_copy(m, i):
         return remote(
@@ -251,61 +259,75 @@
                 def _(side=side, row=row):
                     copy(m, i, side, row).start()
 
-        def grads_g():
-            add_grads(acc, 1, act_g, g2, width)
+        def grads_f():
+            crops = range(M)
+            all_grads(acc, 0, [keep_f[c] for c in crops], [flat(made[c, 3]) for c in crops], width)
+            send_pairs(0, groups // 2)
+
+        last = m == M - 1
 
         await_edges(edge_a_copy, 0)
         await_state(0)
         y1 = flat(state[m, 0])
         upper = jnp.concatenate([edge_a[m, 0, 0], y1, edge_a[m, 1, 0]], 0)
         act_g = jax.nn.silu(upper.astype(F32)).astype(BF16)
-        moved = conv(act_g, taps[1], width, False)
+        keep_g[m] = act_g
+        moved = conv(act_g, taps[1], width)
         await_state(2)
         x2 = (flat(state[m, 2]).astype(F32) - moved).astype(BF16)
         made[m, 2] = x2.reshape(rows, width, channels)
         send_edges(edge_b_copy, 0)
         send_on(m, 2)
 
+        @pl.when(last_sec & (m < M - 2))
+        def _():
+            pl.semaphore_signal(go, inc=1, device_id=(S - 3 - m, r), device_id_type=MESH)
+
         await_edges(edge_a_copy, 1)
         await_state(1)
         g2 = flat(state[m, 1])
         g2_wide = jnp.concatenate([edge_a[m, 0, 1], g2, edge_a[m, 1, 1]], 0)
-        moved = conv(g2_wide, turned[1], width, True) * silu_slope(y1.astype(F32))
+        moved = conv(g2_wide, turned[1], width) * silu_slope(y1.astype(F32))
         await_state(3)
         carried = (flat(state[m, 3]).astype(F32) + moved).astype(BF16)
         made[m, 3] = carried.reshape(rows, width, channels)
         send_edges(edge_b_copy, 1)
         send_on(m, 3)
 
-        @pl.when(m == M - 1)
-        def _():
-            grads_g()
+        @pl.when(last)
+        def _():
+            crops = range(M)
+            all_grads(acc, 1, [keep_g[c] for c in crops], [flat(state[c, 1]) for c in crops], width)
             send_pairs(groups // 2, groups - groups // 2)
 
         await_edges(edge_b_copy, 0)
         lower = jnp.concatenate([edge_b[m, 0, 0], x2, edge_b[m, 1, 0]], 0)
         act_f = jax.nn.silu(lower.astype(F32)).astype(BF16)
-        x1 = (y1.astype(F32) - conv(act_f, taps[0], width, False)).astype(BF16)
+        keep_f[m] = act_f
+
+        @pl.when(last & (s == 0))
+        def _():
+            grads_f()
+
+        x1 = (y1.astype(F32) - conv(act_f, taps[0], width)).astype(BF16)
         made[m, 0] = x1.reshape(rows, width, channels)
         send_edges(edge_a_copy, 0, s > 0)
         send_on(m, 0)
 
         await_edges(edge_b_copy, 1)
         carried_wide = jnp.concatenate([edge_b[m, 0, 1], carried, edge_b[m, 1, 1]], 0)
-        moved = conv(carried_wide, turned[0], width, True) * silu_slope(x2.astype(F32))
+        moved = conv(carried_wide, turned[0], width) * silu_slope(x2.astype(F32))
         made[m, 1] = (g2.astype(F32) + moved).astype(BF16).reshape(rows, width, channels)
         send_edges(edge_a_copy, 1, s > 0)
         send_on(m, 1)
 
-        @pl.when(m < M - 1)
-        def _():
-            grads_g()
-
-        add_grads(acc, 0, act_f, carried, width)
+        @pl.when(last & (s > 0))
+        def _():
+            grads_f()
+
         return carry
 
     lax.fori_loop(0, M, step, 0)
-    send_pairs(0, groups // 2)
     send_sums(groups // 2, groups - groups // 2)
     send_sums(0, groups // 2)
 
@@ -413,19 +435,22 @@
             pltpu.VMEM((M, 4) + shard, BF16),
             pltpu.VMEM((M,) + edge, BF16),
             pltpu.VMEM((M,) + edge, BF16),
+            pltpu.VMEM((M, (rows + 2) * width, channels), BF16),
+            pltpu.VMEM((M, (rows + 2) * width, channels), BF16),
             pltpu.VMEM((4,) + shard, BF16),
             pltpu.VMEM((total, channels), F32),
             pltpu.VMEM((N // 2, chunk, channels), sent),
             pltpu.VMEM((N // 2, chunk, channels), sent),
             pltpu.VMEM((N // 2, chunk, channels), sent),
             pltpu.VMEM((N // 2, chunk, channels), sent),
-            dma((4,)), dma((2, 2)), dma((4,)), dma((2, 2)),
+            dma((4,)), dma((2,)), dma((4,)), dma((2, 2)),
             dma((M, 4)), dma((M, 4)), dma((M, 4)), dma((M, 4)), dma((M, 4)), dma((M, 4)),
             dma((M, 4)), dma((4,)),
             dma((N // 2,)), dma((N // 2,)), dma((N // 2,)), dma((N // 2,)),
+            pltpu.SemaphoreType.REGULAR,
         ],
         compiler_params=pltpu.CompilerParams(
-            collective_id=0, has_side_effects=True, vmem_limit_bytes=64 * 1024 * 1024
+            collective_id=0, has_side_effects=True, vmem_limit_bytes=251 * 256 * 1024
         ),
         cost_estimate=pl.CostEstimate(
             flops=M * 108 * rows * width * channels * channels,

time: 106 us -> 102 us (0.962)
  Pallas kernels: 100 us -> 96.2 us
    pallas_call x1, Pallas kernels: 100 us -> 96.2 us  [local(): pl.pallas_call(functools.partial(body, S, N, scale), out_shape=(jax.Shape...]
where the time goes in v4:
time: 102 us
  Pallas kernels  96.2 us (94%)
  local copies, waits for them, and re-layouts  5.05 us (5%)
    pallas_call x1, Pallas kernels, local(): pl.pallas_call(functools.partial(body, S, N, scale), out_shape=(jax.Shape...  96.2 us
    unnamed x3, local copies, waits for them, and re-layouts  5.05 us

profile of v4, /device:TPU:0, one launch (start us, length us, event | category | flops | bytes accessed | tf_op | source)
XLA Modules:
  0.0 101.8 jit_solution(5043270497709722612)
XLA Ops:
  0.6 96.2 %shard_map.58 = (bf16[1,2,2,64,256]{4,3,2,1,0:T(8,128)(2,1)}, bf16[1,2,2,64,256]{4,3,2,1,0:T(8,128)(2,1)}, f32[1,576,256]{2,1,0:T(8,128)}) custom-call(bf16[1,2,2,64,256]{4,3,2,1,0:T(8,128)(2,1)} %streams.1, bf16[1,2,2,64,256]{4,3,2,1,0:T(8,128)(2,1)} %cotangents.1, bf16[1,1,2,3,3,256,256]{6,5,4,3,2,1,0:T(8,128)(2,1)} %weights_in.1), custom_call_target="tpu_custom_call" | custom-call | flops 3623878656 | bytes 2359296 | tf_op jit(solution)/shard_map/pallas_call | solution.py:421
  96.8 1.6 %copy.9 = bf16[1,2,2,64,256]{4,3,2,1,0:T(8,128)(2,1)} copy(bf16[1,2,2,64,256]{4,3,2,1,0:T(8,128)(2,1)} %get-tuple-element.6) | data formatting | bytes 262144
  98.4 1.6 %copy.10 = bf16[1,2,2,64,256]{4,3,2,1,0:T(8,128)(2,1)} copy(bf16[1,2,2,64,256]{4,3,2,1,0:T(8,128)(2,1)} %get-tuple-element.7) | data formatting | bytes 262144
  99.9 1.9 %copy.11 = f32[1,576,256]{2,1,0:T(8,128)} copy(f32[1,576,256]{2,1,0:T(8,128)} %get-tuple-element.8) | data formatting | bytes 1179648

commit v5 on v4

--- a/solution.py
+++ b/solution.py
@@ -71,9 +71,17 @@
     rows, width, channels = state.shape[2:]
     chunk = terms.shape[1]
     last_sec = s == S - 1
-    below, above = lax.rem(r + 1, N), lax.rem(r + N - 1, N)
-    has_above, has_below = r > 0, r < N - 1
-    sides = ((0, above, has_above), (1, below, has_below))
+
+    def placed(row):
+        return 2 * (row // 2) + lax.rem(row + row // 2, 2)
+
+    def sides_of(row):
+        above, below = placed(lax.rem(row + N - 1, N)), placed(lax.rem(row + 1, N))
+        return ((0, above, row > 0), (1, below, row < N - 1))
+
+    block = placed(r)
+    moved_block = block != r
+    sides, first_sides = sides_of(block), sides_of(r)
     edge_row = (0, rows - 1)
     lower_sec = lax.rem(s + S - 1, S)
     half, group = lax.rem(r, 2), r // 2
@@ -101,19 +109,20 @@
                 ).start()
 
     barrier = pltpu.get_barrier_semaphore()
-    for step in range(S):
-        sec = lax.rem(s + step, S)
-        if step > 0:
-            pl.semaphore_signal(barrier, inc=1, device_id=(sec, r), device_id_type=MESH)
-        for _, row, there in sides:
-            if step > 0:
-                @pl.when(there)
-                def _(sec=sec, row=row):
-                    pl.semaphore_signal(barrier, inc=1, device_id=(sec, row), device_id_type=MESH)
+    pairs = ((group, True), (group - 1, group > 0), (group + 1, group < groups - 1))
     for step in range(1, N):
         pl.semaphore_signal(
             barrier, inc=1, device_id=(s, lax.rem(r + step, N)), device_id_type=MESH
         )
+    for pair, there in pairs:
+        @pl.when(there)
+        def _(pair=pair):
+            for step in range(1, S):
+                for row in range(2):
+                    pl.semaphore_signal(
+                        barrier, inc=1, device_id=(lax.rem(s + step, S), 2 * pair + row),
+                        device_id_type=MESH,
+                    )
 
     for side, _, there in sides:
         @pl.when(jnp.logical_not(there))
@@ -124,12 +133,23 @@
     for load in loads:
         load.wait()
 
-    @pl.when(last_sec)
+    stays = last_sec & jnp.logical_not(moved_block)
+
+    @pl.when(stays)
     def _():
         state[0] = first[...]
 
-    near = 1 + has_above.astype(jnp.int32) + has_below.astype(jnp.int32)
-    pl.semaphore_wait(barrier, (S - 1) * near + N - 1)
+    def away(row):
+        return jnp.logical_not(last_sec & (row == r))
+
+    for side, row, there in first_sides:
+        @pl.when(there & last_sec & (row == r))
+        def _(side=side):
+            for i in range(2):
+                edge_a[0, 1 - side, i] = first[i, edge_row[side]]
+
+    near = 1 + (group > 0).astype(jnp.int32) + (group < groups - 1).astype(jnp.int32)
+    pl.semaphore_wait(barrier, 2 * (S - 1) * near + N - 1)
 
     def first_edge(i, side, row):
         return remote(
@@ -139,7 +159,7 @@
 
     def first_state(i):
         return remote(
-            first.at[i], state.at[own, i], first_send.at[i], st_recv.at[own, i], S - 1, r,
+            first.at[i], state.at[own, i], first_send.at[i], st_recv.at[own, i], S - 1, block,
         )
 
     @pl.when(own >= 2)
@@ -147,12 +167,12 @@
         pl.semaphore_wait(go, 1)
 
     for i in range(2):
-        for side, row, there in sides:
-            @pl.when(there)
+        for side, row, there in first_sides:
+            @pl.when(there & away(row))
             def _(i=i, side=side, row=row):
                 first_edge(i, side, row).start()
 
-    @pl.when(jnp.logical_not(last_sec))
+    @pl.when(jnp.logical_not(stays))
     def _():
         for i in range(4):
             first_state(i).start()
@@ -176,7 +196,7 @@
 
     def result_copy(m, i):
         return remote(
-            made.at[m, i], result.at[i], res_send.at[m, i], res_recv.at[i], S - 1 - m, r,
+            made.at[m, i], result.at[i], res_send.at[m, i], res_recv.at[i], S - 1 - m, block,
         )
 
     def edge_a_copy(m, i, side, row):
@@ -196,7 +216,7 @@
         def _():
             state_copy(m, i).start()
 
-        @pl.when((s == 0) & (m < M - 1))
+        @pl.when((s == 0) & ((m < M - 1) | moved_block))
         def _():
             result_copy(m, i).start()
 
@@ -240,7 +260,7 @@
         return value.reshape(-1, channels)
 
     def step(m, carry):
-        arrives = jnp.logical_not(last_sec & (m == 0))
+        arrives = jnp.logical_not(stays & (m == 0))
 
         def await_state(i):
             @pl.when(arrives)
@@ -249,6 +269,10 @@
 
         def await_edges(copy, i):
             for side, row, there in sides:
+                if copy is edge_a_copy:
+                    here = last_sec & (m == 0) & (block + 2 * side - 1 == r)
+                    there = there & jnp.logical_not(here)
+
                 @pl.when(there)
                 def _(side=side, row=row):
                     copy(m, i, 1 - side, row).wait_recv()
@@ -281,7 +305,7 @@
 
         @pl.when(last_sec & (m < M - 2))
         def _():
-            pl.semaphore_signal(go, inc=1, device_id=(S - 3 - m, r), device_id_type=MESH)
+            pl.semaphore_signal(go, inc=1, device_id=(S - 3 - m, block), device_id_type=MESH)
 
         await_edges(edge_a_copy, 1)
         await_state(1)
@@ -337,23 +361,23 @@
         out_streams[0, 1] = source[2]
         out_grads[0, 0] = source[3]
 
-    @pl.when(s == 0)
+    @pl.when((s == 0) & jnp.logical_not(moved_block))
     def _():
         deliver(made[M - 1])
 
-    @pl.when(s > 0)
+    @pl.when((s > 0) | moved_block)
     def _():
         for i in range(4):
             result_copy(0, i).wait_recv()
         deliver(result[...])
 
-    for side, row, there in sides:
-        @pl.when(there)
+    for side, row, there in first_sides:
+        @pl.when(there & away(row))
         def _(side=side, row=row):
             for i in range(2):
                 first_edge(i, side, row).wait_send()
 
-    @pl.when(jnp.logical_not(last_sec))
+    @pl.when(jnp.logical_not(stays))
     def _():
         for i in range(4):
             first_state(i).wait_send()
@@ -375,7 +399,7 @@
             for i in range(4):
                 state_copy(m, i).wait_send()
 
-        @pl.when((s == 0) & (m < M - 1))
+        @pl.when((s == 0) & ((m < M - 1) | moved_block))
         def _():
             for i in range(4):
                 result_copy(m, i).wait_send()

time: 102 us -> 100 us (0.980)
  Pallas kernels: 96.2 us -> 94.4 us
    pallas_call x1, Pallas kernels: 96.2 us -> 94.4 us  [local(): pl.pallas_call(functools.partial(body, S, N, scale), out_shape=(jax.Shape...]
where the time goes in v5:
time: 100 us
  Pallas kernels  94.4 us (94%)
  local copies, waits for them, and re-layouts  5.05 us (5%)
    pallas_call x1, Pallas kernels, local(): pl.pallas_call(functools.partial(body, S, N, scale), out_shape=(jax.Shape...  94.4 us
    unnamed x3, local copies, waits for them, and re-layouts  5.05 us

profile of v5, /device:TPU:0, one launch (start us, length us, event | category | flops | bytes accessed | tf_op | source)
XLA Modules:
  0.0 100.1 jit_solution(10827405152873647617)
XLA Ops:
  0.6 94.4 %shard_map.58 = (bf16[1,2,2,64,256]{4,3,2,1,0:T(8,128)(2,1)}, bf16[1,2,2,64,256]{4,3,2,1,0:T(8,128)(2,1)}, f32[1,576,256]{2,1,0:T(8,128)}) custom-call(bf16[1,2,2,64,256]{4,3,2,1,0:T(8,128)(2,1)} %streams.1, bf16[1,2,2,64,256]{4,3,2,1,0:T(8,128)(2,1)} %cotangents.1, bf16[1,1,2,3,3,256,256]{6,5,4,3,2,1,0:T(8,128)(2,1)} %weights_in.1), custom_call_target="tpu_custom_call" | custom-call | flops 3623878656 | bytes 2359296 | tf_op jit(solution)/shard_map/pallas_call | solution.py:445
  95.0 1.6 %copy.9 = bf16[1,2,2,64,256]{4,3,2,1,0:T(8,128)(2,1)} copy(bf16[1,2,2,64,256]{4,3,2,1,0:T(8,128)(2,1)} %get-tuple-element.6) | data formatting | bytes 262144
  96.6 1.6 %copy.10 = bf16[1,2,2,64,256]{4,3,2,1,0:T(8,128)(2,1)} copy(bf16[1,2,2,64,256]{4,3,2,1,0:T(8,128)(2,1)} %get-tuple-element.7) | data formatting | bytes 262144
  98.2 1.9 %copy.11 = f32[1,576,256]{2,1,0:T(8,128)} copy(f32[1,576,256]{2,1,0:T(8,128)} %get-tuple-element.8) | data formatting | bytes 1179648

commit v6 on v5

--- a/solution.py
+++ b/solution.py
@@ -12,17 +12,20 @@
 BF16 = jnp.bfloat16
 
 
-def silu_slope(value):
-    sig = jax.nn.sigmoid(value)
+def sigmoid(value):
+    return 0.5 * jnp.tanh(0.5 * value) + 0.5
+
+
+def silu_slope(value, sig):
     return sig + value * sig * (1.0 - sig)
 
 
 def shift_cols(value, by, width):
-    pixels = value.shape[0]
-    col = lax.rem(lax.broadcasted_iota(jnp.int32, value.shape, 0), width)
-    rolled = pltpu.roll(value, by % pixels, axis=0)
+    shaped = value.reshape(-1, width, value.shape[1])
+    rolled = pltpu.roll(shaped, by % width, axis=1)
+    col = lax.broadcasted_iota(jnp.int32, shaped.shape, 1)
     edge = 0 if by > 0 else width - 1
-    return jnp.where(col == edge, 0.0, rolled)
+    return jnp.where(col == edge, 0.0, rolled).reshape(value.shape)
 
 
 def conv(field, kernel, width):
@@ -283,6 +286,11 @@
                 def _(side=side, row=row):
                     copy(m, i, side, row).start()
 
+        def grads_g():
+            crops = range(M)
+            all_grads(acc, 1, [keep_g[c] for c in crops], [flat(state[c, 1]) for c in crops], width)
+            send_pairs(groups // 2, groups - groups // 2)
+
         def grads_f():
             crops = range(M)
             all_grads(acc, 0, [keep_f[c] for c in crops], [flat(made[c, 3]) for c in crops], width)
@@ -294,7 +302,10 @@
         await_state(0)
         y1 = flat(state[m, 0])
         upper = jnp.concatenate([edge_a[m, 0, 0], y1, edge_a[m, 1, 0]], 0)
-        act_g = jax.nn.silu(upper.astype(F32)).astype(BF16)
+        upper = upper.astype(F32)
+        sig = sigmoid(upper)
+        act_g = (upper * sig).astype(BF16)
+        slope = silu_slope(upper[width:-width], sig[width:-width])
         keep_g[m] = act_g
         moved = conv(act_g, taps[1], width)
         await_state(2)
@@ -311,22 +322,23 @@
         await_state(1)
         g2 = flat(state[m, 1])
         g2_wide = jnp.concatenate([edge_a[m, 0, 1], g2, edge_a[m, 1, 1]], 0)
-        moved = conv(g2_wide, turned[1], width) * silu_slope(y1.astype(F32))
+        moved = conv(g2_wide, turned[1], width) * slope
         await_state(3)
         carried = (flat(state[m, 3]).astype(F32) + moved).astype(BF16)
         made[m, 3] = carried.reshape(rows, width, channels)
         send_edges(edge_b_copy, 1)
         send_on(m, 3)
 
-        @pl.when(last)
-        def _():
-            crops = range(M)
-            all_grads(acc, 1, [keep_g[c] for c in crops], [flat(state[c, 1]) for c in crops], width)
-            send_pairs(groups // 2, groups - groups // 2)
+        @pl.when(last & (s == 0))
+        def _():
+            grads_g()
 
         await_edges(edge_b_copy, 0)
         lower = jnp.concatenate([edge_b[m, 0, 0], x2, edge_b[m, 1, 0]], 0)
-        act_f = jax.nn.silu(lower.astype(F32)).astype(BF16)
+        lower = lower.astype(F32)
+        sig = sigmoid(lower)
+        act_f = (lower * sig).astype(BF16)
+        slope = silu_slope(lower[width:-width], sig[width:-width])
         keep_f[m] = act_f
 
         @pl.when(last & (s == 0))
@@ -340,13 +352,14 @@
 
         await_edges(edge_b_copy, 1)
         carried_wide = jnp.concatenate([edge_b[m, 0, 1], carried, edge_b[m, 1, 1]], 0)
-        moved = conv(carried_wide, turned[0], width) * silu_slope(x2.astype(F32))
+        moved = conv(carried_wide, turned[0], width) * slope
         made[m, 1] = (g2.astype(F32) + moved).astype(BF16).reshape(rows, width, channels)
         send_edges(edge_a_copy, 1, s > 0)
         send_on(m, 1)
 
         @pl.when(last & (s > 0))
         def _():
+            grads_g()
             grads_f()
 
         return carry
@@ -474,7 +487,7 @@
             pltpu.SemaphoreType.REGULAR,
         ],
         compiler_params=pltpu.CompilerParams(
-            collective_id=0, has_side_effects=True, vmem_limit_bytes=251 * 256 * 1024
+            collective_id=0, has_side_effects=True, vmem_limit_bytes=52 * 1024 * 1024
         ),
         cost_estimate=pl.CostEstimate(
             flops=M * 108 * rows * width * channels * channels,

time: 100 us -> 103 us (1.030)
  Pallas kernels: 94.4 us -> 98.4 us
  local copies, waits for them, and re-layouts: 5.05 us -> 3.93 us
    pallas_call x1, Pallas kernels: 94.4 us -> 98.4 us  [local(): pl.pallas_call(functools.partial(body, S, N, scale), out_shape=(jax.Shape...]
    unnamed x3 -> x7, local copies, waits for them, and re-layouts: 5.05 us -> 3.93 us
where the time goes in v6:
time: 103 us
  Pallas kernels  98.4 us (96%)
  local copies, waits for them, and re-layouts  3.93 us (4%)
    pallas_call x1, Pallas kernels, local(): pl.pallas_call(functools.partial(body, S, N, scale), out_shape=(jax.Shape...  98.4 us
    unnamed x7, local copies, waits for them, and re-layouts  3.93 us

profile of v6, /device:TPU:0, one launch (start us, length us, event | category | flops | bytes accessed | tf_op | source)
XLA Modules:
  0.0 103.0 jit_solution(3740100678354358692)
XLA Ops:
  0.6 0.0 copy-start
  0.6 0.9 copy-done
  1.5 0.0 copy-start.1
  1.5 0.9 copy-done.1
  2.4 98.4 %shard_map.58 = (bf16[1,2,2,64,256]{4,3,2,1,0:T(8,128)(2,1)S(1)}, bf16[1,2,2,64,256]{4,3,2,1,0:T(8,128)(2,1)S(1)}, f32[1,576,256]{2,1,0:T(8,128)S(1)}) custom-call(bf16[1,2,2,64,256]{4,3,2,1,0:T(8,128)(2,1)S(1)} %copy-done, bf16[1,2,2,64,256]{4,3,2,1,0:T(8,128)(2,1)S(1)} %copy-done.1, bf16[1,1,2,3,3,256,256]{6,5,4,3,2,1,0:T(8,128)(2,1)} %weights_in.1), custom_call_target="tpu_custom_call" | custom-call | flops 3623878656 | bytes 2359296 | tf_op jit(solution)/shard_map/pallas_call | solution.py:458
  100.9 0.7 copy.9
  101.5 0.7 copy.10
  102.2 0.8 copy.11
Async XLA Ops:
  0.6 0.9 copy-start
  1.5 0.9 copy-start.1

commit v7 on v6

--- a/solution.py
+++ b/solution.py
@@ -329,7 +329,7 @@
         send_edges(edge_b_copy, 1)
         send_on(m, 3)
 
-        @pl.when(last & (s == 0))
+        @pl.when(last & (s < 2))
         def _():
             grads_g()
 
@@ -357,9 +357,12 @@
         send_edges(edge_a_copy, 1, s > 0)
         send_on(m, 1)
 
+        @pl.when(last & (s > 1))
+        def _():
+            grads_g()
+
         @pl.when(last & (s > 0))
         def _():
-            grads_g()
             grads_f()
 
         return carry

time: 103 us -> 94.3 us (0.916)
  Pallas kernels: 98.4 us -> 89.1 us
    pallas_call x1, Pallas kernels: 98.4 us -> 89.1 us  [local(): pl.pallas_call(functools.partial(body, S, N, scale), out_shape=(jax.Shape...]
where the time goes in v7:
time: 94.3 us; the launch traced here: 93.6 us
  Pallas kernels  89.1 us (94%)
  local copies, waits for them, and re-layouts  3.93 us (4%)
    pallas_call x1, Pallas kernels, local(): pl.pallas_call(functools.partial(body, S, N, scale), out_shape=(jax.Shape...  89.1 us
    unnamed x7, local copies, waits for them, and re-layouts  3.93 us

profile of v7, /device:TPU:0, one launch (start us, length us, event | category | flops | bytes accessed | tf_op | source)
XLA Modules:
  0.0 93.6 jit_solution(10456089344494887516)
XLA Ops:
  0.6 0.0 copy-start
  0.6 0.9 copy-done
  1.5 0.0 copy-start.1
  1.5 0.9 copy-done.1
  2.4 89.1 %shard_map.58 = (bf16[1,2,2,64,256]{4,3,2,1,0:T(8,128)(2,1)S(1)}, bf16[1,2,2,64,256]{4,3,2,1,0:T(8,128)(2,1)S(1)}, f32[1,576,256]{2,1,0:T(8,128)S(1)}) custom-call(bf16[1,2,2,64,256]{4,3,2,1,0:T(8,128)(2,1)S(1)} %copy-done, bf16[1,2,2,64,256]{4,3,2,1,0:T(8,128)(2,1)S(1)} %copy-done.1, bf16[1,1,2,3,3,256,256]{6,5,4,3,2,1,0:T(8,128)(2,1)} %weights_in.1), custom_call_target="tpu_custom_call" | custom-call | flops 3623878656 | bytes 2359296 | tf_op jit(solution)/shard_map/pallas_call | solution.py:461
  91.5 0.7 copy.9
  92.2 0.7 copy.10
  92.8 0.8 copy.11
Async XLA Ops:
  0.6 0.9 copy-start
  1.5 0.9 copy-start.1

commit v8 on v7

--- a/solution.py
+++ b/solution.py
@@ -321,6 +321,11 @@
         await_edges(edge_a_copy, 1)
         await_state(1)
         g2 = flat(state[m, 1])
+
+        @pl.when(last & (s < 2))
+        def _():
+            grads_g()
+
         g2_wide = jnp.concatenate([edge_a[m, 0, 1], g2, edge_a[m, 1, 1]], 0)
         moved = conv(g2_wide, turned[1], width) * slope
         await_state(3)
@@ -328,10 +333,6 @@
         made[m, 3] = carried.reshape(rows, width, channels)
         send_edges(edge_b_copy, 1)
         send_on(m, 3)
-
-        @pl.when(last & (s < 2))
-        def _():
-            grads_g()
 
         await_edges(edge_b_copy, 0)
         lower = jnp.concatenate([edge_b[m, 0, 0], x2, edge_b[m, 1, 0]], 0)

time: 94.3 us -> 97.8 us (1.037)
  Pallas kernels: 89.1 us -> 92.9 us
    pallas_call x1, Pallas kernels: 89.1 us -> 92.9 us  [local(): pl.pallas_call(functools.partial(body, S, N, scale), out_shape=(jax.Shape...]
where the time goes in v8:
time: 97.8 us; the launch traced here: 97.5 us
  Pallas kernels  92.9 us (95%)
  local copies, waits for them, and re-layouts  3.93 us (4%)
    pallas_call x1, Pallas kernels, local(): pl.pallas_call(functools.partial(body, S, N, scale), out_shape=(jax.Shape...  92.9 us
    unnamed x7, local copies, waits for them, and re-layouts  3.93 us

profile of v8, /device:TPU:0, one launch (start us, length us, event | category | flops | bytes accessed | tf_op | source)
XLA Modules:
  0.0 97.5 jit_solution(11391837820218386240)
XLA Ops:
  0.6 0.0 copy-start
  0.6 0.9 copy-done
  1.5 0.0 copy-start.1
  1.5 0.9 copy-done.1
  2.4 92.9 %shard_map.58 = (bf16[1,2,2,64,256]{4,3,2,1,0:T(8,128)(2,1)S(1)}, bf16[1,2,2,64,256]{4,3,2,1,0:T(8,128)(2,1)S(1)}, f32[1,576,256]{2,1,0:T(8,128)S(1)}) custom-call(bf16[1,2,2,64,256]{4,3,2,1,0:T(8,128)(2,1)S(1)} %copy-done, bf16[1,2,2,64,256]{4,3,2,1,0:T(8,128)(2,1)S(1)} %copy-done.1, bf16[1,1,2,3,3,256,256]{6,5,4,3,2,1,0:T(8,128)(2,1)} %weights_in.1), custom_call_target="tpu_custom_call" | custom-call | flops 3623878656 | bytes 2359296 | tf_op jit(solution)/shard_map/pallas_call | solution.py:462
  95.4 0.7 copy.9
  96.0 0.7 copy.10
  96.7 0.8 copy.11
Async XLA Ops:
  0.6 0.9 copy-start
  1.5 0.9 copy-start.1
